TPU v7x, 256 devices: a whole 4x4x8 slice. The times are simulated.
256 devices in a mesh: seq: 16 (over y, x_hi, core), tp: 16 (over x_lo, z).
Axes of the slice: x: 4 (x_hi: 2, x_lo: 2; x = x_hi * 2 + x_lo), y: 4, z: 8, core: 2. Of those that a mesh axis runs over, the one named last changes fastest.
Arguments:
- tokens: bfloat16 [8192, 4096], P('seq', 'tp'), may hold values from -24 to 24
- query_weight: bfloat16 [4096, 4096], P(None, 'tp'), may hold values from -0.09375 to 0.09375
- kv_weight: bfloat16 [2, 4096, 1024], P(None, 'seq'), may hold values from -0.09375 to 0.09375
- out_weight: bfloat16 [4096, 4096], P('tp'), may hold values from -0.75 to 0.75
Outputs:
- attended: bfloat16 [8192, 4096], P('seq', 'tp')
All inputs are finite; a program needn't handle non-finite values.
Results may differ from a plain program's by a relative error of at most 0.024.
Values may be sent and summed in bfloat16 or wider, within the bound.
No kernel may reach another device: no remote copies, remote signals or barrier semaphores. Data moves between devices by JAX's collectives and lax.ppermute only.
A program may use at most 64 MiB of HBM per device.

v0:
```python
import functools

import jax
import jax.numpy as jnp
from jax import lax
from jax.experimental import pallas as pl
from jax.experimental.pallas import tpu as pltpu
from jax.sharding import PartitionSpec as P

HEADS = 32
KV_HEADS = 8
HD = 128
ROTARY_BASE = 500000.0
MASKED = -1e30
BOTH = ("seq", "tp")
NY, NH, NC, NL, NZ = 4, 2, 2, 2, 8
NX = NH * NL
BLOCK = 256
ARRIVAL = (0, 1, 7, 2, 6, 3, 5, 4)
ORDER = (4, 5, 3, 6, 0, 2, 7, 1)


def linear(y, h, c, l, z):
    return ((y * NH + h) * NC + c) * (NL * NZ) + l * NZ + z


def routes(move):
    pairs = []
    for y in range(NY):
        for h in range(NH):
            for c in range(NC):
                for l in range(NL):
                    for z in range(NZ):
                        pairs.append((linear(y, h, c, l, z), linear(*move(y, h, c, l, z))))
    return pairs


def sign_of(core):
    return 1 if core == 0 else -1


def swap_route(shift):
    return routes(lambda y, h, c, l, z: (y, h, l, c, (z + sign_of(l) * shift) % NZ))


def swap_back_route(shift):
    return routes(lambda y, h, c, l, z: (y, h, l, c, (z + sign_of(c) * shift) % NZ))


def z_chain(shift):
    return routes(lambda y, h, c, l, z: (y, h, c, l, (z + sign_of(c) * shift) % NZ))


def y_chain(shift):
    return routes(lambda y, h, c, l, z: ((y + sign_of(c) * shift) % NY, h, c, l, z))


def z_route(shift):
    return routes(lambda y, h, c, l, z: (y, h, c, l, (z + shift) % NZ))


def y_route(shift):
    return routes(lambda y, h, c, l, z: ((y + shift) % NY, h, c, l, z))


def x_route(shift):
    def move(y, h, c, l, z):
        x = (h * NL + l + shift) % NX
        return y, x // NL, c, x % NL, z

    return routes(move)


def line_route(shift):
    over_x, over_y = x_route(shift), y_route(shift)
    return routes_by_core(over_x, over_y)


def cross_route(shift):
    over_x, over_y = x_route(shift), y_route(shift)
    return routes_by_core(over_y, over_x)


def routes_by_core(first, second):
    pairs = []
    for one, other in zip(first, second):
        core = one[0] // (NL * NZ) % NC
        pairs.append(one if core == 0 else other)
    return pairs


CORE_ROUTE = routes(lambda y, h, c, l, z: (y, h, 1 - c, l, z))
PAIR_ROUTE = routes(lambda y, h, c, l, z: (y, h, c, 1 - l, z))
FLIP_ROUTE = routes(lambda y, h, c, l, z: (y, 1 - h, c, 1 - l, z))


def send(value, route):
    return lax.ppermute(value, BOTH, route)


SWAP = [(source, target) for source, target in swap_route(0) if source != target]


def send_swapped(value, same):
    return jnp.where(same, value, send(value, SWAP))


def rotated(vectors, cos, sin):
    half = HD // 2
    turned = jnp.concatenate([vectors[:, half:], vectors[:, :half]], 1)
    return vectors * cos + turned * sin


def project_rows(place, blocks, weight_of):
    c, z = place[2], place[4]
    acc = None
    for steps in ARRIVAL:
        for j in range(2):
            core = c if j == 0 else 1 - c
            feature = core * NZ + lax.rem(z + (2 * core - 1) * steps + NZ, NZ)
            part = jnp.dot(
                blocks[2 * steps + j][...],
                weight_of(feature),
                preferred_element_type=jnp.float32,
            )
            acc = part if acc is None else acc + part
    return acc


def project_kv_kernel(place, *refs):
    blocks, parts = refs[: 2 * NZ], refs[2 * NZ : 2 * NZ + 4]
    cosine, sine, out, wkv = refs[2 * NZ + 4 :]
    y, h, c = place[0], place[1], place[2]
    at = 0
    for part in parts:
        count = part.shape[0]
        wkv[at : at + count] = part[...]
        at += count

    def weight_of(feature):
        dy = lax.rem((2 * c - 1) * (feature // 4 - y) + NY, NY)
        dh = lax.rem(lax.rem(feature // 2, 2) + h, 2)
        dc = lax.rem(lax.rem(feature, 2) + c, 2)
        return wkv[(dy * 2 + dh) * 2 + dc]

    acc = project_rows(place, blocks, weight_of)
    out[:, :HD] = rotated(acc[:, :HD], cosine[...], sine[...]).astype(jnp.bfloat16)
    out[:, HD:] = acc[:, HD:].astype(jnp.bfloat16)


def project_q_kernel(rows, place, *refs):
    blocks = refs[: 2 * NZ]
    own_wq, moved_wq = refs[2 * NZ : 2 * NZ + 2]
    cosine, sine, out, wq, sem = refs[2 * NZ + 2 :]
    c, l = place[2], place[3]
    fetch_own = pltpu.make_async_copy(own_wq, wq, sem)
    fetch_moved = pltpu.make_async_copy(moved_wq, wq, sem)

    @pl.when(c == l)
    def _():
        fetch_own.start()

    @pl.when(c != l)
    def _():
        fetch_moved.start()

    fetch_own.wait()

    def weight_of(feature):
        return wq[pl.ds(pl.multiple_of(feature * BLOCK, BLOCK), BLOCK), :]

    acc = project_rows(place, blocks, weight_of)
    scale = HD**-0.5 * 1.4426950408889634
    for head in range(2):
        turned = rotated(acc[:, head * HD : (head + 1) * HD], cosine[...], sine[...])
        out[head * rows : (head + 1) * rows] = (turned * scale).astype(jnp.bfloat16)


VMEM = pl.BlockSpec(memory_space=pltpu.VMEM)
SMEM = pl.BlockSpec(memory_space=pltpu.SMEM)
ANYWHERE = pl.BlockSpec(memory_space=pl.ANY)
PARAMS = pltpu.CompilerParams(vmem_limit_bytes=48 * 2**20)


def order_kernel(place, weight, near, last):
    c, z = place[2], place[4]
    for at, steps in enumerate(ORDER):
        column = lax.rem(z + (1 - 2 * c) * steps + NZ, NZ)
        piece = weight[:, pl.ds(pl.multiple_of(column * BLOCK, BLOCK), BLOCK)]
        if at < 5:
            near[:, at * BLOCK : (at + 1) * BLOCK] = piece
        else:
            last[:, (at - 5) * BLOCK : (at - 4) * BLOCK] = piece


def order_columns(place, weight):
    rows = weight.shape[0]
    return pl.pallas_call(
        order_kernel,
        out_shape=(
            jax.ShapeDtypeStruct((rows, 5 * BLOCK), weight.dtype),
            jax.ShapeDtypeStruct((rows, 3 * BLOCK), weight.dtype),
        ),
        in_specs=[SMEM, VMEM],
        out_specs=(VMEM, VMEM),
        compiler_params=PARAMS,
        cost_estimate=pl.CostEstimate(flops=0, bytes_accessed=2 * 2**20, transcendentals=0),
    )(place, weight)


def project_kv(place, blocks, parts, cosine, sine):
    rows = blocks[0].shape[0]
    return pl.pallas_call(
        project_kv_kernel,
        out_shape=jax.ShapeDtypeStruct((rows, 2 * HD), jnp.bfloat16),
        in_specs=[SMEM] + [VMEM] * (len(blocks) + len(parts) + 2),
        out_specs=VMEM,
        scratch_shapes=[pltpu.VMEM((16, BLOCK, 2 * HD), jnp.bfloat16)],
        compiler_params=PARAMS,
        cost_estimate=pl.CostEstimate(
            flops=2 * rows * 4096 * 2 * HD, bytes_accessed=6 * 2**20, transcendentals=0
        ),
    )(place, *blocks, *parts, cosine, sine)


def project_q(place, blocks, own_wq, moved_wq, cosine, sine):
    rows = blocks[0].shape[0]
    return pl.pallas_call(
        functools.partial(project_q_kernel, rows),
        out_shape=jax.ShapeDtypeStruct((2 * rows, HD), jnp.bfloat16),
        in_specs=[SMEM] + [VMEM] * len(blocks) + [ANYWHERE] * 2 + [VMEM] * 2,
        out_specs=VMEM,
        scratch_shapes=[pltpu.VMEM(own_wq.shape, jnp.bfloat16), pltpu.SemaphoreType.DMA],
        compiler_params=PARAMS,
        cost_estimate=pl.CostEstimate(
            flops=2 * rows * 4096 * 2 * HD, bytes_accessed=6 * 2**20, transcendentals=0
        ),
    )(place, *blocks, own_wq, moved_wq, cosine, sine)


def attend_kernel(rows, steps, first, last, place, query, *refs):
    lines = refs[: len(steps)]
    refs = refs[len(steps) :]
    if not first:
        old_state, refs = refs[:3], refs[3:]
    if last:
        out, held, top, total, acc = refs
    else:
        top, total, acc, held = refs
    y, c, x = place[0], place[2], place[5]
    mine = y * NX + x

    def merge(keys, values, begin):
        scores = lax.dot_general(
            query[...], keys, (((1,), (1,)), ((), ())), preferred_element_type=jnp.float32
        )
        if begin:
            query_at = lax.rem(lax.broadcasted_iota(jnp.int32, scores.shape, 0), rows)
            key_at = lax.broadcasted_iota(jnp.int32, scores.shape, 1)
            scores = jnp.where(key_at <= query_at, scores, MASKED)
            peak = jnp.max(scores, axis=1, keepdims=True)
            peak = jnp.broadcast_to(peak, (2 * rows, HD))
        else:
            old = top[...]
            peak = jnp.maximum(old, jnp.max(scores, axis=1, keepdims=True))
        weights = jnp.exp2(scores - jnp.concatenate([peak] * (rows // HD), 1))
        sums = jnp.sum(weights, axis=1, keepdims=True)
        part = jnp.dot(weights.astype(jnp.bfloat16), values, preferred_element_type=jnp.float32)
        if begin:
            total[...] = jnp.broadcast_to(sums, (2 * rows, HD))
            acc[...] = part
        else:
            factor = jnp.exp2(old - peak)
            total[...] = total[...] * factor + sums
            acc[...] = acc[...] * factor + part
        top[...] = peak

    if not first:
        for new, old in zip((top, total, acc), old_state):
            new[...] = old[...]
    if first:
        merge(lines[0][0, :, :HD], lines[0][0, :, HD:], True)
    count = sum(line.shape[0] for line in lines)

    def step(block, carry):
        outer, inner, start = 0, 0, 0
        for line, (away, begin) in zip(lines, steps):
            here = (block >= start) & (block < start + line.shape[0])
            outer = jnp.where(here, away, outer)
            inner = jnp.where(here, lax.rem(4 + start - begin - block + 4, 4), inner)
            start += line.shape[0]
        dy = jnp.where(c == 0, outer, inner)
        dx = jnp.where(c == 0, inner, outer)
        theirs = lax.rem(y + dy, NY) * NX + lax.rem(x + dx, NX)

        @pl.when(theirs < mine)
        def _():
            start = 0
            for line in lines:

                @pl.when((block >= start) & (block < start + line.shape[0]))
                def _(line=line, start=start):
                    held[...] = line[block - start]

                start += line.shape[0]
            merge(held[:, :HD], held[:, HD:], False)

        return carry

    lax.fori_loop(1 if first else 0, count, step, 0)
    if last:
        context = acc[...] / total[...]
        out[...] = jnp.concatenate([context[:rows], context[rows:]], 1).astype(jnp.bfloat16)


def attend(place, query, lines, steps, state, last):
    rows = query.shape[0] // 2
    count = sum(line.shape[0] for line in lines)
    wide = (2 * rows, HD)
    scratch = [pltpu.VMEM((rows, 2 * HD), jnp.bfloat16)]
    if last:
        out_shape = jax.ShapeDtypeStruct((rows, 2 * HD), jnp.bfloat16)
        out_specs = VMEM
        scratch += [pltpu.VMEM(wide, jnp.float32)] * 3
    else:
        out_shape = (jax.ShapeDtypeStruct(wide, jnp.float32),) * 3
        out_specs = (VMEM,) * 3
    return pl.pallas_call(
        functools.partial(attend_kernel, rows, steps, not state, last),
        out_shape=out_shape,
        in_specs=[SMEM, VMEM] + [VMEM] * (len(lines) + len(state)),
        out_specs=out_specs,
        scratch_shapes=scratch,
        compiler_params=PARAMS,
        cost_estimate=pl.CostEstimate(
            flops=4 * 2 * rows * count * rows * HD,
            bytes_accessed=count * rows * 4 * HD,
            transcendentals=2 * rows * count * rows,
        ),
    )(place, query, *lines, *state)


def gather_inputs(tokens, query_weight, kv_weight, out_weight, place, c, z, same):
    def columns(core):
        part = lax.dynamic_slice_in_dim(kv_weight, (core * 4 + z // 2) * HD, HD, 2)
        return jnp.concatenate([part[0], part[1]], 1)

    mine, other = columns(c), columns(1 - c)
    own = [None] * NZ
    own[1] = send(tokens, swap_route(1))
    own[7] = send(tokens, swap_route(-1))
    own[0] = send_swapped(tokens, same)
    flipped = send(jnp.stack([mine, other]), FLIP_ROUTE)
    own[0], own[1], own[7], flipped, query_weight, out_weight = lax.optimization_barrier(
        (own[0], own[1], own[7], flipped, query_weight, out_weight)
    )
    others = send(jnp.stack([other, flipped[1]]), CORE_ROUTE)
    four = jnp.stack([mine, others[0], flipped[0], others[1]])
    first = send(four, y_chain(1))
    second = send(four, y_chain(-1))
    moved_wq = send(query_weight, SWAP)
    own[2] = send(own[1], z_chain(1))
    own[6] = send(own[7], z_chain(-1))
    own[3] = send(own[2], z_chain(1))
    own[5] = send(own[6], z_chain(-1))
    own[3], own[5], first, second = lax.optimization_barrier((own[3], own[5], first, second))
    far = send(first, y_chain(1))
    own[4] = send(own[3], z_chain(1))
    blocks = []
    for block in own:
        blocks += [block, send(block, CORE_ROUTE)]
    half_columns = out_weight.shape[1] // 2
    wo = lax.dynamic_slice_in_dim(out_weight, c * half_columns, half_columns, 1)
    near, last = order_columns(place, wo)
    moved_near = send(near, PAIR_ROUTE)
    far, moved_wq, last = lax.optimization_barrier((far, moved_wq, last))
    return blocks, [four, first, far, second], query_weight, moved_wq, near, moved_near, last


def scatter_sums(part_of, same):
    def add(part, arrived):
        return (part + arrived.astype(jnp.float32)).astype(jnp.bfloat16)

    long = send(part_of(4).astype(jnp.bfloat16), z_chain(1))
    short = send(part_of(5).astype(jnp.bfloat16), z_chain(-1))
    long = send(add(part_of(3), long), z_chain(1))
    short = send(add(part_of(6), short), z_chain(-1))
    middle = send_swapped(part_of(0).astype(jnp.bfloat16), same)
    long, short, middle = lax.optimization_barrier((long, short, middle))
    long = send(add(part_of(2), long), z_chain(1))
    short = send(add(part_of(7), short), swap_back_route(-1))
    long = send(add(part_of(1), long), swap_back_route(1))
    total = middle.astype(jnp.float32) + short.astype(jnp.float32) + long.astype(jnp.float32)
    return total.astype(jnp.bfloat16)


def shards(tokens, query_weight, kv_weight, out_weight):
    rows = tokens.shape[0]
    seq_rank = lax.axis_index("seq")
    tp_rank = lax.axis_index("tp")
    y, h, c = seq_rank // 4, (seq_rank // 2) % 2, seq_rank % 2
    l, z = tp_rank // NZ, tp_rank % NZ
    x = h * NL + l
    place = jnp.stack([y, h, c, l, z, x]).astype(jnp.int32)
    same = c == l

    blocks, wkv_parts, query_weight, moved_wq, near, moved_near, last = gather_inputs(
        tokens, query_weight, kv_weight, out_weight, place, c, z, same
    )

    positions = ((y * NX + x) * rows + jnp.arange(rows, dtype=jnp.int32)).astype(jnp.float32)
    frequency = ROTARY_BASE ** (-jnp.arange(HD // 2, dtype=jnp.float32) / (HD // 2))
    angles = positions[:, None] * frequency[None, :]
    cosine, sine = jnp.cos(angles), jnp.sin(angles)
    cosine = jnp.concatenate([cosine, cosine], 1)
    sine = jnp.concatenate([-sine, sine], 1)

    block = project_kv(place, blocks, wkv_parts, cosine, sine)
    line_first = send(block, line_route(1))
    line_second = send(block, line_route(-1))
    line_first, moved_near = lax.optimization_barrier((line_first, moved_near))
    line_far = send(line_first, line_route(1))
    query = project_q(place, blocks, query_weight, moved_wq, cosine, sine)
    line_far, line_second, query = lax.optimization_barrier((line_far, line_second, query))
    line = jnp.stack([block, line_first, line_far, line_second])
    first = send(line, cross_route(1))
    second = send(line, cross_route(-1))
    state = attend(place, query, [line], ((0, 0),), (), False)
    first, second, state = lax.optimization_barrier((first, second, state))
    far_low = send(first[:2], cross_route(1))
    far_high = send(second[2:], cross_route(-1))

    state = attend(place, query, [first, second], ((3, 0), (1, 0)), state, False)
    context = attend(place, query, [far_low, far_high], ((2, 0), (2, 2)), state, True)
    last, near, moved_near, context = lax.optimization_barrier((last, near, moved_near, context))
    near = jnp.concatenate([near, moved_near], 0)
    last = jnp.concatenate([last, send(last, PAIR_ROUTE)], 0)
    other = send(context, CORE_ROUTE)
    context = jnp.concatenate(
        [jnp.where(same, context, other), jnp.where(same, other, context)], 1
    )

    def part_of(steps):
        at = ORDER.index(steps)
        piece, at = (near, at * BLOCK) if at < 5 else (last, (at - 5) * BLOCK)
        return jnp.dot(context, piece[:, at : at + BLOCK], preferred_element_type=jnp.float32)

    return scatter_sums(part_of, same)


def solution(mesh):
    return jax.shard_map(
        shards,
        mesh=mesh,
        in_specs=(P("seq", "tp"), P(None, "tp"), P(None, "seq", None), P("tp", None)),
        out_specs=P("seq", "tp"),
        check_vma=False,
    )
```

profile of v0, /device:TPU:20, one launch (start us, length us, event | category | flops | bytes accessed | tf_op | source)
XLA Modules:
  0.0 145.6 jit_solution(1410838503173221590)
XLA Ops:
  4.4 1.9 %collective-permute-start.1 = (bf16[512,256]{1,0:T(8,128)(2,1)}, bf16[512,256]{1,0:T(8,128)(2,1)S(1)}, u32[]{:S(2)}, u32[]{:S(2)}) collective-permute-start(bf16[512,256]{1,0:T(8,128)(2,1)} %param.4), channel_id=1, source_target_pairs={{0,1},{1,2},{2,3},{3,4},{4,5},{5,6},{6,7},{7,0},{8,23},{9,16},{10,... | collective-permute-start | bytes 786440 | tf_op jit(solution)/shard_map/ppermute | solution.py:98
  6.3 3.9 %collective-permute-start.2 = (bf16[512,256]{1,0:T(8,128)(2,1)}, bf16[512,256]{1,0:T(8,128)(2,1)S(1)}, u32[]{:S(2)}, u32[]{:S(2)}) collective-permute-start(bf16[512,256]{1,0:T(8,128)(2,1)} %param.4), channel_id=1, source_target_pairs={{0,7},{1,0},{2,1},{3,2},{4,3},{5,4},{6,5},{7,6},{8,17},{9,18},{10,... | collective-permute-start | bytes 786440 | tf_op jit(solution)/shard_map/ppermute | solution.py:98
  11.7 5.9 %collective-permute-done.1.refs_2_ = bf16[512,256]{1,0:T(8,128)(2,1)S(1)} collective-permute-done((bf16[512,256]{1,0:T(8,128)(2,1)}, bf16[512,256]{1,0:T(8,128)(2,1)S(1)}, u32[]{:S(2)}, u32[]{:S(2)}) %collective-permute-start.1) | collective-permute-done | bytes 262176 | tf_op jit(solution)/shard_map/ppermute | solution.py:98
  17.5 2.0 %collective-permute-start.12 = (bf16[4096,256]{1,0:T(8,128)(2,1)}, bf16[4096,256]{1,0:T(8,128)(2,1)}, u32[]{:S(2)}, u32[]{:S(2)}) collective-permute-start(bf16[4096,256]{1,0:T(8,128)(2,1)} %refs_16_), channel_id=1, source_target_pairs={{8,16},{9,17},{10,18},{11,19},{12,20},{13,21},{14,22},{15,23},{16,... | collective-permute-start | bytes 6291464 | tf_op jit(solution)/shard_map/ppermute | solution.py:98
  19.6 3.1 %collective-permute-start.8 = (bf16[2,256,256]{2,1,0:T(8,128)(2,1)S(1)}, bf16[2,256,256]{2,1,0:T(8,128)(2,1)S(1)}, u32[]{:S(2)}, u32[]{:S(2)}) collective-permute-start(bf16[2,256,256]{2,1,0:T(8,128)(2,1)S(1)} %pad_maximum_fusion.4), channel_id=1, source_target_pairs={{0,16},{1,17},{2,18},{3,19},{4,20},{5,21},{6,22},{7,23},{8,24},{9,... | collective-permute-start | bytes 786440 | tf_op jit(solution)/shard_map/ppermute | solution.py:98
  22.7 3.2 %collective-permute-start.6 = (bf16[512,256]{1,0:T(8,128)(2,1)S(1)}, bf16[512,256]{1,0:T(8,128)(2,1)S(1)}, u32[]{:S(2)}, u32[]{:S(2)}) collective-permute-start(bf16[512,256]{1,0:T(8,128)(2,1)S(1)} %collective-permute-done.2.refs_14_), channel_id=1, source_target_pairs={{0,7},{1,0},{2,1},{3,2},{4,3},{5,4},{6,5},{7,6},{8,15},{9,8},{10,9... | collective-permute-start | bytes 786440 | tf_op jit(solution)/shard_map/ppermute | solution.py:98
  26.5 1.6 %collective-permute-start.9 = (bf16[4,256,256]{2,1,0:T(8,128)(2,1)S(1)}, bf16[4,256,256]{2,1,0:T(8,128)(2,1)}, u32[]{:S(2)}, u32[]{:S(2)}) collective-permute-start(bf16[4,256,256]{2,1,0:T(8,128)(2,1)S(1)} %pad_maximum_fusion.1.refs_16_), channel_id=1, source_target_pairs={{0,64},{1,65},{2,66},{3,67},{4,68},{5,69},{6,70},{7,71},{8,72},{9,... | collective-permute-start | bytes 1572872 | tf_op jit(solution)/shard_map/ppermute | solution.py:98
  28.1 4.2 %collective-permute-done.4.refs_4_ = bf16[512,256]{1,0:T(8,128)(2,1)S(1)} collective-permute-done((bf16[512,256]{1,0:T(8,128)(2,1)S(1)}, bf16[512,256]{1,0:T(8,128)(2,1)S(1)}, u32[]{:S(2)}, u32[]{:S(2)}) %collective-permute-start.4) | collective-permute-done | bytes 262176 | tf_op jit(solution)/shard_map/ppermute | solution.py:98
  32.4 3.2 %collective-permute-start.7 = (bf16[512,256]{1,0:T(8,128)(2,1)S(1)}, bf16[512,256]{1,0:T(8,128)(2,1)S(1)}, u32[]{:S(2)}, u32[]{:S(2)}) collective-permute-start(bf16[512,256]{1,0:T(8,128)(2,1)S(1)} %collective-permute-done.6.refs_12_), channel_id=1, source_target_pairs={{0,7},{1,0},{2,1},{3,2},{4,3},{5,4},{6,5},{7,6},{8,15},{9,8},{10,9... | collective-permute-start | bytes 786440 | tf_op jit(solution)/shard_map/ppermute | solution.py:98
  35.6 6.7 %collective-permute-done.5.refs_6_ = bf16[512,256]{1,0:T(8,128)(2,1)S(1)} collective-permute-done((bf16[512,256]{1,0:T(8,128)(2,1)S(1)}, bf16[512,256]{1,0:T(8,128)(2,1)S(1)}, u32[]{:S(2)}, u32[]{:S(2)}) %collective-permute-start.5) | collective-permute-done | bytes 262176 | tf_op jit(solution)/shard_map/ppermute | solution.py:98
  43.6 1.6 %collective-permute-start.11 = (bf16[4,256,256]{2,1,0:T(8,128)(2,1)}, bf16[4,256,256]{2,1,0:T(8,128)(2,1)}, u32[]{:S(2)}, u32[]{:S(2)}) collective-permute-start(bf16[4,256,256]{2,1,0:T(8,128)(2,1)} %collective-permute-done.9.refs_17_), channel_id=1, source_target_pairs={{0,64},{1,65},{2,66},{3,67},{4,68},{5,69},{6,70},{7,71},{8,72},{9,... | collective-permute-start | bytes 1572872 | tf_op jit(solution)/shard_map/ppermute | solution.py:98
  47.6 6.0 %collective-permute-done.17.refs_8_ = bf16[512,256]{1,0:T(8,128)(2,1)} collective-permute-done((bf16[512,256]{1,0:T(8,128)(2,1)}, bf16[512,256]{1,0:T(8,128)(2,1)}, u32[]{:S(2)}, u32[]{:S(2)}) %collective-permute-start.17) | collective-permute-done | bytes 262176 | tf_op jit(solution)/shard_map/ppermute | solution.py:98
  56.1 3.2 %shard_map.47 = bf16[512,256]{1,0:T(8,128)(2,1)S(1)} custom-call(s32[6]{0:T(128)S(1)} %stack.64.place, bf16[512,256]{1,0:T(8,128)(2,1)S(1)} %broadcast_select_fusion.3.refs_0_, bf16[512,256]{1,0:T(8,128)(2,1)} %collective-permute-done.13.refs_1_, bf16[512,256]{1,0:T(8,128)(2,1)S(1)} %collective-permute-done.1.refs_2_, ...), custom_call_target="tpu_custom_call" | custom-call | flops 1073741824 | bytes 6291456 | tf_op jit(solution)/shard_map/pallas_call | solution.py:213
  59.4 2.0 %collective-permute-start.25 = (bf16[512,256]{1,0:T(8,128)(2,1)S(1)}, bf16[512,256]{1,0:T(8,128)(2,1)S(1)}, u32[]{:S(2)}, u32[]{:S(2)}) collective-permute-start(bf16[512,256]{1,0:T(8,128)(2,1)S(1)} %shard_map.47), channel_id=1, source_target_pairs={{0,40},{1,41},{2,42},{3,43},{4,44},{5,45},{6,46},{7,47},{8,0},{9,1... | collective-permute-start | bytes 786440 | tf_op jit(solution)/shard_map/ppermute | solution.py:98
  61.4 2.2 %collective-permute-done.23 = bf16[256,1280]{1,0:T(8,128)(2,1)S(1)} collective-permute-done((bf16[256,1280]{1,0:T(8,128)(2,1)S(1)}, bf16[256,1280]{1,0:T(8,128)(2,1)S(1)}, u32[]{:S(2)}, u32[]{:S(2)}) %collective-permute-start.23) | collective-permute-done | bytes 655392 | tf_op jit(solution)/shard_map/ppermute | solution.py:98
  63.7 2.1 %collective-permute-done.22 = bf16[512,256]{1,0:T(8,128)(2,1)S(1)} collective-permute-done((bf16[512,256]{1,0:T(8,128)(2,1)S(1)}, bf16[512,256]{1,0:T(8,128)(2,1)S(1)}, u32[]{:S(2)}, u32[]{:S(2)}) %collective-permute-start.22) | collective-permute-done | bytes 262176 | tf_op jit(solution)/shard_map/ppermute | solution.py:98
  66.9 4.2 %shard_map.48.query = bf16[1024,128]{1,0:T(8,128)(2,1)S(1)} custom-call(s32[6]{0:T(128)S(1)} %stack.64.place, bf16[512,256]{1,0:T(8,128)(2,1)S(1)} %broadcast_select_fusion.3.refs_0_, bf16[512,256]{1,0:T(8,128)(2,1)} %collective-permute-done.13.refs_1_, bf16[512,256]{1,0:T(8,128)(2,1)S(1)} %collective-permute-done.1.refs_2_, ...), custom_call_target="tpu_custom_call" | custom-call | flops 1073741824 | bytes 6291456 | tf_op jit(solution)/shard_map/pallas_call | solution.py:228
  74.4 3.5 %shard_map.49 = (f32[1024,128]{1,0:T(8,128)S(1)}, f32[1024,128]{1,0:T(8,128)S(1)}, f32[1024,128]{1,0:T(8,128)S(1)}) custom-call(s32[6]{0:T(128)S(1)} %stack.64.place, bf16[1024,128]{1,0:T(8,128)(2,1)S(1)} %shard_map.48.query, bf16[4,512,256]{2,1,0:T(8,128)(2,1)S(1)} %pad_maximum_fusion.refs_0_), custom_call_target="tpu_custom_call" | custom-call | flops 1073741824 | bytes 1048576 | tf_op jit(solution)/shard_map/pallas_call | solution.py:328
  77.9 9.3 %collective-permute-done.26.refs_0_ = bf16[4,512,256]{2,1,0:T(8,128)(2,1)S(1)} collective-permute-done((bf16[4,512,256]{2,1,0:T(8,128)(2,1)S(1)}, bf16[4,512,256]{2,1,0:T(8,128)(2,1)S(1)}, u32[]{:S(2)}, u32[]{:S(2)}) %collective-permute-start.26) | collective-permute-done | bytes 1048608 | tf_op jit(solution)/shard_map/ppermute | solution.py:98
  87.9 3.4 %collective-permute-start.28 = (bf16[2,512,256]{2,1,0:T(8,128)(2,1)S(1)}, bf16[2,512,256]{2,1,0:T(8,128)(2,1)S(1)}, u32[]{:S(2)}, u32[]{:S(2)}) collective-permute-start(bf16[2,512,256]{2,1,0:T(8,128)(2,1)S(1)} %slice.62), channel_id=1, source_target_pairs={{0,64},{1,65},{2,66},{3,67},{4,68},{5,69},{6,70},{7,71},{8,72},{9,... | collective-permute-start | bytes 1572872 | tf_op jit(solution)/shard_map/ppermute | solution.py:98
  91.5 4.3 %shard_map.50 = (f32[1024,128]{1,0:T(8,128)S(1)}, f32[1024,128]{1,0:T(8,128)S(1)}, f32[1024,128]{1,0:T(8,128)S(1)}) custom-call(s32[6]{0:T(128)S(1)} %stack.64.place, bf16[1024,128]{1,0:T(8,128)(2,1)S(1)} %shard_map.48.query, bf16[4,512,256]{2,1,0:T(8,128)(2,1)S(1)} %collective-permute-done.26.refs_0_, ...), custom_call_target="tpu_custom_call" | custom-call | flops 2147483648 | bytes 2097152 | tf_op jit(solution)/shard_map/pallas_call | solution.py:328
  95.8 2.3 %collective-permute-done.28.refs_0_ = bf16[2,512,256]{2,1,0:T(8,128)(2,1)S(1)} collective-permute-done((bf16[2,512,256]{2,1,0:T(8,128)(2,1)S(1)}, bf16[2,512,256]{2,1,0:T(8,128)(2,1)S(1)}, u32[]{:S(2)}, u32[]{:S(2)}) %collective-permute-start.28) | collective-permute-done | bytes 524320 | tf_op jit(solution)/shard_map/ppermute | solution.py:98
  98.0 2.6 %collective-permute-done.29.refs_1_ = bf16[2,512,256]{2,1,0:T(8,128)(2,1)S(1)} collective-permute-done((bf16[2,512,256]{2,1,0:T(8,128)(2,1)S(1)}, bf16[2,512,256]{2,1,0:T(8,128)(2,1)S(1)}, u32[]{:S(2)}, u32[]{:S(2)}) %collective-permute-start.29) | collective-permute-done | bytes 524320 | tf_op jit(solution)/shard_map/ppermute | solution.py:98
  100.6 4.2 %shard_map.51 = bf16[512,256]{1,0:T(8,128)(2,1)S(1)} custom-call(s32[6]{0:T(128)S(1)} %stack.64.place, bf16[1024,128]{1,0:T(8,128)(2,1)S(1)} %shard_map.48.query, bf16[2,512,256]{2,1,0:T(8,128)(2,1)S(1)} %collective-permute-done.28.refs_0_, bf16[2,512,256]{2,1,0:T(8,128)(2,1)S(1)} %collective-permute-done.29.refs_1_, ...), custom_call_target="tpu_custom_call" | custom-call | flops 1073741824 | bytes 1048576 | tf_op jit(solution)/shard_map/pallas_call | solution.py:328
  104.9 1.7 %collective-permute-start.36 = (bf16[256,768]{1,0:T(8,128)(2,1)S(1)}, bf16[256,768]{1,0:T(8,128)(2,1)S(1)}, u32[]{:S(2)}, u32[]{:S(2)}) collective-permute-start(bf16[256,768]{1,0:T(8,128)(2,1)S(1)} %get-tuple-element.78), channel_id=1, source_target_pairs={{0,8},{1,9},{2,10},{3,11},{4,12},{5,13},{6,14},{7,15},{8,0},{9,1},... | collective-permute-start | bytes 1179656 | tf_op jit(solution)/shard_map/ppermute | solution.py:98
  109.3 1.7 %collective-permute-start.31 = (bf16[512,256]{1,0:T(8,128)(2,1)S(1)}, bf16[512,256]{1,0:T(8,128)(2,1)S(1)}, u32[]{:S(2)}, u32[]{:S(2)}) collective-permute-start(bf16[512,256]{1,0:T(8,128)(2,1)S(1)} %convolution_convert_fusion.2), channel_id=1, source_target_pairs={{0,1},{1,2},{2,3},{3,4},{4,5},{5,6},{6,7},{7,0},{8,9},{9,10},{10,1... | collective-permute-start | bytes 786440 | tf_op jit(solution)/shard_map/ppermute | solution.py:98
  111.9 5.4 %collective-permute-done.33 = bf16[512,256]{1,0:T(8,128)(2,1)S(1)} collective-permute-done((bf16[512,256]{1,0:T(8,128)(2,1)S(1)}, bf16[512,256]{1,0:T(8,128)(2,1)S(1)}, u32[]{:S(2)}, u32[]{:S(2)}) %collective-permute-start.33) | collective-permute-done | bytes 262176 | tf_op jit(solution)/shard_map/ppermute | solution.py:98
  118.4 1.7 %collective-permute-start.32 = (bf16[512,256]{1,0:T(8,128)(2,1)S(1)}, bf16[512,256]{1,0:T(8,128)(2,1)S(1)}, u32[]{:S(2)}, u32[]{:S(2)}) collective-permute-start(bf16[512,256]{1,0:T(8,128)(2,1)S(1)} %fusion), channel_id=1, source_target_pairs={{0,1},{1,2},{2,3},{3,4},{4,5},{5,6},{6,7},{7,0},{8,9},{9,10},{10,1... | collective-permute-start | bytes 786440 | tf_op jit(solution)/shard_map/ppermute | solution.py:98
  120.1 5.5 %collective-permute-done.34 = bf16[512,256]{1,0:T(8,128)(2,1)S(1)} collective-permute-done((bf16[512,256]{1,0:T(8,128)(2,1)S(1)}, bf16[512,256]{1,0:T(8,128)(2,1)S(1)}, u32[]{:S(2)}, u32[]{:S(2)}) %collective-permute-start.34) | collective-permute-done | bytes 262176 | tf_op jit(solution)/shard_map/ppermute | solution.py:98
  127.1 3.2 %collective-permute-start.37 = (bf16[512,256]{1,0:T(8,128)(2,1)S(1)}, bf16[512,256]{1,0:T(8,128)(2,1)S(1)}, u32[]{:S(2)}, u32[]{:S(2)}) collective-permute-start(bf16[512,256]{1,0:T(8,128)(2,1)S(1)} %fusion.2), channel_id=1, source_target_pairs={{0,7},{1,0},{2,1},{3,2},{4,3},{5,4},{6,5},{7,6},{8,23},{9,16},{10,... | collective-permute-start | bytes 786440 | tf_op jit(solution)/shard_map/ppermute | solution.py:98
  130.3 6.6 %collective-permute-done.38 = bf16[512,256]{1,0:T(8,128)(2,1)S(1)} collective-permute-done((bf16[512,256]{1,0:T(8,128)(2,1)S(1)}, bf16[512,256]{1,0:T(8,128)(2,1)S(1)}, u32[]{:S(2)}, u32[]{:S(2)}) %collective-permute-start.38) | collective-permute-done | bytes 262176 | tf_op jit(solution)/shard_map/ppermute | solution.py:98
  137.3 7.6 %collective-permute-done.39 = bf16[512,256]{1,0:T(8,128)(2,1)S(1)} collective-permute-done((bf16[512,256]{1,0:T(8,128)(2,1)S(1)}, bf16[512,256]{1,0:T(8,128)(2,1)S(1)}, u32[]{:S(2)}, u32[]{:S(2)}) %collective-permute-start.39) | collective-permute-done | bytes 262176 | tf_op jit(solution)/shard_map/ppermute | solution.py:98
  (107 shorter events, 25.3 us)
Async XLA Ops:
  0.0 10.3 %collective-permute-start = (bf16[512,256]{1,0:T(8,128)(2,1)}, bf16[512,256]{1,0:T(8,128)(2,1)}, u32[]{:S(2)}, u32[]{:S(2)}) collective-permute-start(bf16[512,256]{1,0:T(8,128)(2,1)} %param.4), channel_id=1, source_target_pairs={{8,16},{9,17},{10,18},{11,19},{12,20},{13,21},{14,22},{15,23},{16,... | collective-permute-start | bytes 786440 | tf_op jit(solution)/shard_map/ppermute | solution.py:98
  3.2 8.4 %collective-permute-start.3 = (bf16[2,256,256]{2,1,0:T(8,128)(2,1)}, bf16[2,256,256]{2,1,0:T(8,128)(2,1)S(1)}, u32[]{:S(2)}, u32[]{:S(2)}) collective-permute-start(bf16[2,256,256]{2,1,0:T(8,128)(2,1)} %pad_maximum_fusion.3), channel_id=1, source_target_pairs={{0,40},{1,41},{2,42},{3,43},{4,44},{5,45},{6,46},{7,47},{8,32},{9,... | collective-permute-start | bytes 786440 | tf_op jit(solution)/shard_map/ppermute | solution.py:98
  4.4 13.1 %collective-permute-start.1 = (bf16[512,256]{1,0:T(8,128)(2,1)}, bf16[512,256]{1,0:T(8,128)(2,1)S(1)}, u32[]{:S(2)}, u32[]{:S(2)}) collective-permute-start(bf16[512,256]{1,0:T(8,128)(2,1)} %param.4), channel_id=1, source_target_pairs={{0,1},{1,2},{2,3},{3,4},{4,5},{5,6},{6,7},{7,0},{8,23},{9,16},{10,... | collective-permute-start | bytes 786440 | tf_op jit(solution)/shard_map/ppermute | solution.py:98
  6.3 11.2 %collective-permute-start.2 = (bf16[512,256]{1,0:T(8,128)(2,1)}, bf16[512,256]{1,0:T(8,128)(2,1)S(1)}, u32[]{:S(2)}, u32[]{:S(2)}) collective-permute-start(bf16[512,256]{1,0:T(8,128)(2,1)} %param.4), channel_id=1, source_target_pairs={{0,7},{1,0},{2,1},{3,2},{4,3},{5,4},{6,5},{7,6},{8,17},{9,18},{10,... | collective-permute-start | bytes 786440 | tf_op jit(solution)/shard_map/ppermute | solution.py:98
  17.5 36.6 %collective-permute-start.12 = (bf16[4096,256]{1,0:T(8,128)(2,1)}, bf16[4096,256]{1,0:T(8,128)(2,1)}, u32[]{:S(2)}, u32[]{:S(2)}) collective-permute-start(bf16[4096,256]{1,0:T(8,128)(2,1)} %refs_16_), channel_id=1, source_target_pairs={{8,16},{9,17},{10,18},{11,19},{12,20},{13,21},{14,22},{15,23},{16,... | collective-permute-start | bytes 6291464 | tf_op jit(solution)/shard_map/ppermute | solution.py:98
  19.6 6.3 %collective-permute-start.8 = (bf16[2,256,256]{2,1,0:T(8,128)(2,1)S(1)}, bf16[2,256,256]{2,1,0:T(8,128)(2,1)S(1)}, u32[]{:S(2)}, u32[]{:S(2)}) collective-permute-start(bf16[2,256,256]{2,1,0:T(8,128)(2,1)S(1)} %pad_maximum_fusion.4), channel_id=1, source_target_pairs={{0,16},{1,17},{2,18},{3,19},{4,20},{5,21},{6,22},{7,23},{8,24},{9,... | collective-permute-start | bytes 786440 | tf_op jit(solution)/shard_map/ppermute | solution.py:98
  22.7 9.7 %collective-permute-start.4 = (bf16[512,256]{1,0:T(8,128)(2,1)S(1)}, bf16[512,256]{1,0:T(8,128)(2,1)S(1)}, u32[]{:S(2)}, u32[]{:S(2)}) collective-permute-start(bf16[512,256]{1,0:T(8,128)(2,1)S(1)} %collective-permute-done.1.refs_2_), channel_id=1, source_target_pairs={{0,1},{1,2},{2,3},{3,4},{4,5},{5,6},{6,7},{7,0},{8,9},{9,10},{10,1... | collective-permute-start | bytes 786440 | tf_op jit(solution)/shard_map/ppermute | solution.py:98
  22.7 9.7 %collective-permute-start.6 = (bf16[512,256]{1,0:T(8,128)(2,1)S(1)}, bf16[512,256]{1,0:T(8,128)(2,1)S(1)}, u32[]{:S(2)}, u32[]{:S(2)}) collective-permute-start(bf16[512,256]{1,0:T(8,128)(2,1)S(1)} %collective-permute-done.2.refs_14_), channel_id=1, source_target_pairs={{0,7},{1,0},{2,1},{3,2},{4,3},{5,4},{6,5},{7,6},{8,15},{9,8},{10,9... | collective-permute-start | bytes 786440 | tf_op jit(solution)/shard_map/ppermute | solution.py:98
  26.0 16.8 %collective-permute-start.10 = (bf16[4,256,256]{2,1,0:T(8,128)(2,1)S(1)}, bf16[4,256,256]{2,1,0:T(8,128)(2,1)S(1)}, u32[]{:S(2)}, u32[]{:S(2)}) collective-permute-start(bf16[4,256,256]{2,1,0:T(8,128)(2,1)S(1)} %pad_maximum_fusion.1.refs_16_), channel_id=1, source_target_pairs={{0,192},{1,193},{2,194},{3,195},{4,196},{5,197},{6,198},{7,199},{8... | collective-permute-start | bytes 1572872 | tf_op jit(solution)/shard_map/ppermute | solution.py:98
  26.5 16.3 %collective-permute-start.9 = (bf16[4,256,256]{2,1,0:T(8,128)(2,1)S(1)}, bf16[4,256,256]{2,1,0:T(8,128)(2,1)}, u32[]{:S(2)}, u32[]{:S(2)}) collective-permute-start(bf16[4,256,256]{2,1,0:T(8,128)(2,1)S(1)} %pad_maximum_fusion.1.refs_16_), channel_id=1, source_target_pairs={{0,64},{1,65},{2,66},{3,67},{4,68},{5,69},{6,70},{7,71},{8,72},{9,... | collective-permute-start | bytes 1572872 | tf_op jit(solution)/shard_map/ppermute | solution.py:98
  32.4 9.9 %collective-permute-start.5 = (bf16[512,256]{1,0:T(8,128)(2,1)S(1)}, bf16[512,256]{1,0:T(8,128)(2,1)S(1)}, u32[]{:S(2)}, u32[]{:S(2)}) collective-permute-start(bf16[512,256]{1,0:T(8,128)(2,1)S(1)} %collective-permute-done.4.refs_4_), channel_id=1, source_target_pairs={{0,1},{1,2},{2,3},{3,4},{4,5},{5,6},{6,7},{7,0},{8,9},{9,10},{10,1... | collective-permute-start | bytes 786440 | tf_op jit(solution)/shard_map/ppermute | solution.py:98
  32.4 9.9 %collective-permute-start.7 = (bf16[512,256]{1,0:T(8,128)(2,1)S(1)}, bf16[512,256]{1,0:T(8,128)(2,1)S(1)}, u32[]{:S(2)}, u32[]{:S(2)}) collective-permute-start(bf16[512,256]{1,0:T(8,128)(2,1)S(1)} %collective-permute-done.6.refs_12_), channel_id=1, source_target_pairs={{0,7},{1,0},{2,1},{3,2},{4,3},{5,4},{6,5},{7,6},{8,15},{9,8},{10,9... | collective-permute-start | bytes 786440 | tf_op jit(solution)/shard_map/ppermute | solution.py:98
  43.6 10.0 %collective-permute-start.11 = (bf16[4,256,256]{2,1,0:T(8,128)(2,1)}, bf16[4,256,256]{2,1,0:T(8,128)(2,1)}, u32[]{:S(2)}, u32[]{:S(2)}) collective-permute-start(bf16[4,256,256]{2,1,0:T(8,128)(2,1)} %collective-permute-done.9.refs_17_), channel_id=1, source_target_pairs={{0,64},{1,65},{2,66},{3,67},{4,68},{5,69},{6,70},{7,71},{8,72},{9,... | collective-permute-start | bytes 1572872 | tf_op jit(solution)/shard_map/ppermute | solution.py:98
  45.7 7.9 %collective-permute-start.17 = (bf16[512,256]{1,0:T(8,128)(2,1)}, bf16[512,256]{1,0:T(8,128)(2,1)}, u32[]{:S(2)}, u32[]{:S(2)}) collective-permute-start(bf16[512,256]{1,0:T(8,128)(2,1)} %copy-done.5), channel_id=1, source_target_pairs={{0,1},{1,2},{2,3},{3,4},{4,5},{5,6},{6,7},{7,0},{8,9},{9,10},{10,1... | collective-permute-start | bytes 786440 | tf_op jit(solution)/shard_map/ppermute | solution.py:98
  46.8 16.8 %collective-permute-start.23 = (bf16[256,1280]{1,0:T(8,128)(2,1)S(1)}, bf16[256,1280]{1,0:T(8,128)(2,1)S(1)}, u32[]{:S(2)}, u32[]{:S(2)}) collective-permute-start(bf16[256,1280]{1,0:T(8,128)(2,1)S(1)} %get-tuple-element.75), channel_id=1, source_target_pairs={{0,8},{1,9},{2,10},{3,11},{4,12},{5,13},{6,14},{7,15},{8,0},{9,1},... | collective-permute-start | bytes 1966088 | tf_op jit(solution)/shard_map/ppermute | solution.py:98
  47.4 8.0 %collective-permute-start.20 = (bf16[512,256]{1,0:T(8,128)(2,1)S(1)}, bf16[512,256]{1,0:T(8,128)(2,1)S(1)}, u32[]{:S(2)}, u32[]{:S(2)}) collective-permute-start(bf16[512,256]{1,0:T(8,128)(2,1)S(1)} %copy-done.4), channel_id=1, source_target_pairs={{0,16},{1,17},{2,18},{3,19},{4,20},{5,21},{6,22},{7,23},{8,24},{9,... | collective-permute-start | bytes 786440 | tf_op jit(solution)/shard_map/ppermute | solution.py:98
  59.3 6.4 %collective-permute-start.22 = (bf16[512,256]{1,0:T(8,128)(2,1)S(1)}, bf16[512,256]{1,0:T(8,128)(2,1)S(1)}, u32[]{:S(2)}, u32[]{:S(2)}) collective-permute-start(bf16[512,256]{1,0:T(8,128)(2,1)S(1)} %shard_map.47), channel_id=1, source_target_pairs={{0,8},{1,9},{2,10},{3,11},{4,12},{5,13},{6,14},{7,15},{8,32},{9,33... | collective-permute-start | bytes 786440 | tf_op jit(solution)/shard_map/ppermute | solution.py:98
  59.4 11.7 %collective-permute-start.25 = (bf16[512,256]{1,0:T(8,128)(2,1)S(1)}, bf16[512,256]{1,0:T(8,128)(2,1)S(1)}, u32[]{:S(2)}, u32[]{:S(2)}) collective-permute-start(bf16[512,256]{1,0:T(8,128)(2,1)S(1)} %shard_map.47), channel_id=1, source_target_pairs={{0,40},{1,41},{2,42},{3,43},{4,44},{5,45},{6,46},{7,47},{8,0},{9,1... | collective-permute-start | bytes 786440 | tf_op jit(solution)/shard_map/ppermute | solution.py:98
  65.8 6.4 %collective-permute-start.24 = (bf16[512,256]{1,0:T(8,128)(2,1)S(1)}, bf16[512,256]{1,0:T(8,128)(2,1)S(1)}, u32[]{:S(2)}, u32[]{:S(2)}) collective-permute-start(bf16[512,256]{1,0:T(8,128)(2,1)S(1)} %collective-permute-done.22), channel_id=1, source_target_pairs={{0,8},{1,9},{2,10},{3,11},{4,12},{5,13},{6,14},{7,15},{8,32},{9,33... | collective-permute-start | bytes 786440 | tf_op jit(solution)/shard_map/ppermute | solution.py:98
  72.3 14.9 %collective-permute-start.26 = (bf16[4,512,256]{2,1,0:T(8,128)(2,1)S(1)}, bf16[4,512,256]{2,1,0:T(8,128)(2,1)S(1)}, u32[]{:S(2)}, u32[]{:S(2)}) collective-permute-start(bf16[4,512,256]{2,1,0:T(8,128)(2,1)S(1)} %pad_maximum_fusion.refs_0_), channel_id=1, source_target_pairs={{0,64},{1,65},{2,66},{3,67},{4,68},{5,69},{6,70},{7,71},{8,72},{9,... | collective-permute-start | bytes 3145736 | tf_op jit(solution)/shard_map/ppermute | solution.py:98
  73.1 14.8 %collective-permute-start.27 = (bf16[4,512,256]{2,1,0:T(8,128)(2,1)S(1)}, bf16[4,512,256]{2,1,0:T(8,128)(2,1)S(1)}, u32[]{:S(2)}, u32[]{:S(2)}) collective-permute-start(bf16[4,512,256]{2,1,0:T(8,128)(2,1)S(1)} %pad_maximum_fusion.refs_0_), channel_id=1, source_target_pairs={{0,192},{1,193},{2,194},{3,195},{4,196},{5,197},{6,198},{7,199},{8... | collective-permute-start | bytes 3145736 | tf_op jit(solution)/shard_map/ppermute | solution.py:98
  87.9 10.1 %collective-permute-start.28 = (bf16[2,512,256]{2,1,0:T(8,128)(2,1)S(1)}, bf16[2,512,256]{2,1,0:T(8,128)(2,1)S(1)}, u32[]{:S(2)}, u32[]{:S(2)}) collective-permute-start(bf16[2,512,256]{2,1,0:T(8,128)(2,1)S(1)} %slice.62), channel_id=1, source_target_pairs={{0,64},{1,65},{2,66},{3,67},{4,68},{5,69},{6,70},{7,71},{8,72},{9,... | collective-permute-start | bytes 1572872 | tf_op jit(solution)/shard_map/ppermute | solution.py:98
  91.4 9.3 %collective-permute-start.29 = (bf16[2,512,256]{2,1,0:T(8,128)(2,1)S(1)}, bf16[2,512,256]{2,1,0:T(8,128)(2,1)S(1)}, u32[]{:S(2)}, u32[]{:S(2)}) collective-permute-start(bf16[2,512,256]{2,1,0:T(8,128)(2,1)S(1)} %slice.63), channel_id=1, source_target_pairs={{0,192},{1,193},{2,194},{3,195},{4,196},{5,197},{6,198},{7,199},{8... | collective-permute-start | bytes 1572872 | tf_op jit(solution)/shard_map/ppermute | solution.py:98
  104.9 15.2 %collective-permute-start.36 = (bf16[256,768]{1,0:T(8,128)(2,1)S(1)}, bf16[256,768]{1,0:T(8,128)(2,1)S(1)}, u32[]{:S(2)}, u32[]{:S(2)}) collective-permute-start(bf16[256,768]{1,0:T(8,128)(2,1)S(1)} %get-tuple-element.78), channel_id=1, source_target_pairs={{0,8},{1,9},{2,10},{3,11},{4,12},{5,13},{6,14},{7,15},{8,0},{9,1},... | collective-permute-start | bytes 1179656 | tf_op jit(solution)/shard_map/ppermute | solution.py:98
  108.4 8.8 %collective-permute-start.33 = (bf16[512,256]{1,0:T(8,128)(2,1)S(1)}, bf16[512,256]{1,0:T(8,128)(2,1)S(1)}, u32[]{:S(2)}, u32[]{:S(2)}) collective-permute-start(bf16[512,256]{1,0:T(8,128)(2,1)S(1)} %convolution_convert_fusion.1), channel_id=1, source_target_pairs={{0,7},{1,0},{2,1},{3,2},{4,3},{5,4},{6,5},{7,6},{8,15},{9,8},{10,9... | collective-permute-start | bytes 786440 | tf_op jit(solution)/shard_map/ppermute | solution.py:98
  109.3 8.8 %collective-permute-start.31 = (bf16[512,256]{1,0:T(8,128)(2,1)S(1)}, bf16[512,256]{1,0:T(8,128)(2,1)S(1)}, u32[]{:S(2)}, u32[]{:S(2)}) collective-permute-start(bf16[512,256]{1,0:T(8,128)(2,1)S(1)} %convolution_convert_fusion.2), channel_id=1, source_target_pairs={{0,1},{1,2},{2,3},{3,4},{4,5},{5,6},{6,7},{7,0},{8,9},{9,10},{10,1... | collective-permute-start | bytes 786440 | tf_op jit(solution)/shard_map/ppermute | solution.py:98
  111.2 8.9 %collective-permute-start.35 = (bf16[512,256]{1,0:T(8,128)(2,1)S(1)}, bf16[512,256]{1,0:T(8,128)(2,1)S(1)}, u32[]{:S(2)}, u32[]{:S(2)}) collective-permute-start(bf16[512,256]{1,0:T(8,128)(2,1)S(1)} %convolution_convert_fusion), channel_id=1, source_target_pairs={{8,16},{9,17},{10,18},{11,19},{12,20},{13,21},{14,22},{15,23},{16,... | collective-permute-start | bytes 786440 | tf_op jit(solution)/shard_map/ppermute | solution.py:98
  117.6 8.0 %collective-permute-start.34 = (bf16[512,256]{1,0:T(8,128)(2,1)S(1)}, bf16[512,256]{1,0:T(8,128)(2,1)S(1)}, u32[]{:S(2)}, u32[]{:S(2)}) collective-permute-start(bf16[512,256]{1,0:T(8,128)(2,1)S(1)} %fusion.1), channel_id=1, source_target_pairs={{0,7},{1,0},{2,1},{3,2},{4,3},{5,4},{6,5},{7,6},{8,15},{9,8},{10,9... | collective-permute-start | bytes 786440 | tf_op jit(solution)/shard_map/ppermute | solution.py:98
  118.4 7.9 %collective-permute-start.32 = (bf16[512,256]{1,0:T(8,128)(2,1)S(1)}, bf16[512,256]{1,0:T(8,128)(2,1)S(1)}, u32[]{:S(2)}, u32[]{:S(2)}) collective-permute-start(bf16[512,256]{1,0:T(8,128)(2,1)S(1)} %fusion), channel_id=1, source_target_pairs={{0,1},{1,2},{2,3},{3,4},{4,5},{5,6},{6,7},{7,0},{8,9},{9,10},{10,1... | collective-permute-start | bytes 786440 | tf_op jit(solution)/shard_map/ppermute | solution.py:98
  126.6 10.3 %collective-permute-start.38 = (bf16[512,256]{1,0:T(8,128)(2,1)S(1)}, bf16[512,256]{1,0:T(8,128)(2,1)S(1)}, u32[]{:S(2)}, u32[]{:S(2)}) collective-permute-start(bf16[512,256]{1,0:T(8,128)(2,1)S(1)} %fusion.4), channel_id=1, source_target_pairs={{0,1},{1,2},{2,3},{3,4},{4,5},{5,6},{6,7},{7,0},{8,9},{9,10},{10,1... | collective-permute-start | bytes 786440 | tf_op jit(solution)/shard_map/ppermute | solution.py:98
  127.1 10.2 %collective-permute-start.37 = (bf16[512,256]{1,0:T(8,128)(2,1)S(1)}, bf16[512,256]{1,0:T(8,128)(2,1)S(1)}, u32[]{:S(2)}, u32[]{:S(2)}) collective-permute-start(bf16[512,256]{1,0:T(8,128)(2,1)S(1)} %fusion.2), channel_id=1, source_target_pairs={{0,7},{1,0},{2,1},{3,2},{4,3},{5,4},{6,5},{7,6},{8,23},{9,16},{10,... | collective-permute-start | bytes 786440 | tf_op jit(solution)/shard_map/ppermute | solution.py:98
  137.2 7.7 %collective-permute-start.39 = (bf16[512,256]{1,0:T(8,128)(2,1)S(1)}, bf16[512,256]{1,0:T(8,128)(2,1)S(1)}, u32[]{:S(2)}, u32[]{:S(2)}) collective-permute-start(bf16[512,256]{1,0:T(8,128)(2,1)S(1)} %fusion.3), channel_id=1, source_target_pairs={{0,1},{1,2},{2,3},{3,4},{4,5},{5,6},{6,7},{7,0},{8,17},{9,18},{10,... | collective-permute-start | bytes 786440 | tf_op jit(solution)/shard_map/ppermute | solution.py:98
  (18 other events, 113.1 us)
where the time goes:
time: 148 us; the launch traced here: 146 us
  waiting for transfers between devices  72.3 us (49%)
  starting transfers between devices  44.1 us (30%)
  Pallas kernels  20.1 us (14%)
  other arithmetic  4.08 us (3%)
  matrix products  2.35 us (2%)
  local copies, waits for them, and re-layouts  2.18 us (1%)
    ppermute x40, waiting for transfers between devices, send(): return lax.ppermute(value, BOTH, route)  72.3 us
    ppermute x40, starting transfers between devices, send(): return lax.ppermute(value, BOTH, route)  44.1 us
    pallas_call x3, Pallas kernels, attend(): pl.pallas_call(functools.partial(attend_kernel, rows, steps, not state, l...  12 us
    pallas_call x1, Pallas kernels, project_q(): pl.pallas_call(functools.partial(project_q_kernel, rows), out_shape=jax.S...  4.21 us
    pallas_call x1, Pallas kernels, project_kv(): pl.pallas_call(project_kv_kernel, out_shape=jax.ShapeDtypeStruct((rows, 2...  3.22 us
  transfers between devices with their start and end apart: 40, of which 23 were waited for; matrix products, arithmetic and copies ran while one was open for 4% of the time, Pallas kernels for 11%

commit v1 on v0

--- a/solution.py
+++ b/solution.py
@@ -363,9 +363,9 @@
     own[6] = send(own[7], z_chain(-1))
     own[3] = send(own[2], z_chain(1))
     own[5] = send(own[6], z_chain(-1))
+    own[4] = send(own[3], z_chain(1))
     own[3], own[5], first, second = lax.optimization_barrier((own[3], own[5], first, second))
     far = send(first, y_chain(1))
-    own[4] = send(own[3], z_chain(1))
     blocks = []
     for block in own:
         blocks += [block, send(block, CORE_ROUTE)]

time: 148 us -> 148 us (level)
  no operation moved by 1% of the time
where the time goes in v1:
time: 148 us; the launch traced here: 146 us
  waiting for transfers between devices  72.3 us (49%)
  starting transfers between devices  44.1 us (30%)
  Pallas kernels  20.1 us (14%)
  other arithmetic  4.08 us (3%)
  matrix products  2.35 us (2%)
  local copies, waits for them, and re-layouts  2.18 us (1%)
    ppermute x40, waiting for transfers between devices, send(): return lax.ppermute(value, BOTH, route)  72.3 us
    ppermute x40, starting transfers between devices, send(): return lax.ppermute(value, BOTH, route)  44.1 us
    pallas_call x3, Pallas kernels, attend(): pl.pallas_call(functools.partial(attend_kernel, rows, steps, not state, l...  12 us
    pallas_call x1, Pallas kernels, project_q(): pl.pallas_call(functools.partial(project_q_kernel, rows), out_shape=jax.S...  4.21 us
    pallas_call x1, Pallas kernels, project_kv(): pl.pallas_call(project_kv_kernel, out_shape=jax.ShapeDtypeStruct((rows, 2...  3.22 us
  transfers between devices with their start and end apart: 40, of which 23 were waited for; matrix products, arithmetic and copies ran while one was open for 4% of the time, Pallas kernels for 11%

profile of v1, /device:TPU:20, one launch (start us, length us, event | category | flops | bytes accessed | tf_op | source)
XLA Modules:
  0.0 145.6 jit_solution(1410838503173221590)
XLA Ops:
  4.4 1.9 %collective-permute-start.1 = (bf16[512,256]{1,0:T(8,128)(2,1)}, bf16[512,256]{1,0:T(8,128)(2,1)S(1)}, u32[]{:S(2)}, u32[]{:S(2)}) collective-permute-start(bf16[512,256]{1,0:T(8,128)(2,1)} %param.4), channel_id=1, source_target_pairs={{0,1},{1,2},{2,3},{3,4},{4,5},{5,6},{6,7},{7,0},{8,23},{9,16},{10,... | collective-permute-start | bytes 786440 | tf_op jit(solution)/shard_map/ppermute | solution.py:98
  6.3 3.9 %collective-permute-start.2 = (bf16[512,256]{1,0:T(8,128)(2,1)}, bf16[512,256]{1,0:T(8,128)(2,1)S(1)}, u32[]{:S(2)}, u32[]{:S(2)}) collective-permute-start(bf16[512,256]{1,0:T(8,128)(2,1)} %param.4), channel_id=1, source_target_pairs={{0,7},{1,0},{2,1},{3,2},{4,3},{5,4},{6,5},{7,6},{8,17},{9,18},{10,... | collective-permute-start | bytes 786440 | tf_op jit(solution)/shard_map/ppermute | solution.py:98
  11.7 5.9 %collective-permute-done.1.refs_2_ = bf16[512,256]{1,0:T(8,128)(2,1)S(1)} collective-permute-done((bf16[512,256]{1,0:T(8,128)(2,1)}, bf16[512,256]{1,0:T(8,128)(2,1)S(1)}, u32[]{:S(2)}, u32[]{:S(2)}) %collective-permute-start.1) | collective-permute-done | bytes 262176 | tf_op jit(solution)/shard_map/ppermute | solution.py:98
  17.5 2.0 %collective-permute-start.12 = (bf16[4096,256]{1,0:T(8,128)(2,1)}, bf16[4096,256]{1,0:T(8,128)(2,1)}, u32[]{:S(2)}, u32[]{:S(2)}) collective-permute-start(bf16[4096,256]{1,0:T(8,128)(2,1)} %refs_16_), channel_id=1, source_target_pairs={{8,16},{9,17},{10,18},{11,19},{12,20},{13,21},{14,22},{15,23},{16,... | collective-permute-start | bytes 6291464 | tf_op jit(solution)/shard_map/ppermute | solution.py:98
  19.6 3.1 %collective-permute-start.8 = (bf16[2,256,256]{2,1,0:T(8,128)(2,1)S(1)}, bf16[2,256,256]{2,1,0:T(8,128)(2,1)S(1)}, u32[]{:S(2)}, u32[]{:S(2)}) collective-permute-start(bf16[2,256,256]{2,1,0:T(8,128)(2,1)S(1)} %pad_maximum_fusion.4), channel_id=1, source_target_pairs={{0,16},{1,17},{2,18},{3,19},{4,20},{5,21},{6,22},{7,23},{8,24},{9,... | collective-permute-start | bytes 786440 | tf_op jit(solution)/shard_map/ppermute | solution.py:98
  22.7 3.2 %collective-permute-start.6 = (bf16[512,256]{1,0:T(8,128)(2,1)S(1)}, bf16[512,256]{1,0:T(8,128)(2,1)S(1)}, u32[]{:S(2)}, u32[]{:S(2)}) collective-permute-start(bf16[512,256]{1,0:T(8,128)(2,1)S(1)} %collective-permute-done.2.refs_14_), channel_id=1, source_target_pairs={{0,7},{1,0},{2,1},{3,2},{4,3},{5,4},{6,5},{7,6},{8,15},{9,8},{10,9... | collective-permute-start | bytes 786440 | tf_op jit(solution)/shard_map/ppermute | solution.py:98
  26.5 1.6 %collective-permute-start.9 = (bf16[4,256,256]{2,1,0:T(8,128)(2,1)S(1)}, bf16[4,256,256]{2,1,0:T(8,128)(2,1)}, u32[]{:S(2)}, u32[]{:S(2)}) collective-permute-start(bf16[4,256,256]{2,1,0:T(8,128)(2,1)S(1)} %pad_maximum_fusion.1.refs_16_), channel_id=1, source_target_pairs={{0,64},{1,65},{2,66},{3,67},{4,68},{5,69},{6,70},{7,71},{8,72},{9,... | collective-permute-start | bytes 1572872 | tf_op jit(solution)/shard_map/ppermute | solution.py:98
  28.1 4.2 %collective-permute-done.4.refs_4_ = bf16[512,256]{1,0:T(8,128)(2,1)S(1)} collective-permute-done((bf16[512,256]{1,0:T(8,128)(2,1)S(1)}, bf16[512,256]{1,0:T(8,128)(2,1)S(1)}, u32[]{:S(2)}, u32[]{:S(2)}) %collective-permute-start.4) | collective-permute-done | bytes 262176 | tf_op jit(solution)/shard_map/ppermute | solution.py:98
  32.4 3.2 %collective-permute-start.7 = (bf16[512,256]{1,0:T(8,128)(2,1)S(1)}, bf16[512,256]{1,0:T(8,128)(2,1)S(1)}, u32[]{:S(2)}, u32[]{:S(2)}) collective-permute-start(bf16[512,256]{1,0:T(8,128)(2,1)S(1)} %collective-permute-done.6.refs_12_), channel_id=1, source_target_pairs={{0,7},{1,0},{2,1},{3,2},{4,3},{5,4},{6,5},{7,6},{8,15},{9,8},{10,9... | collective-permute-start | bytes 786440 | tf_op jit(solution)/shard_map/ppermute | solution.py:98
  35.6 6.7 %collective-permute-done.5.refs_6_ = bf16[512,256]{1,0:T(8,128)(2,1)S(1)} collective-permute-done((bf16[512,256]{1,0:T(8,128)(2,1)S(1)}, bf16[512,256]{1,0:T(8,128)(2,1)S(1)}, u32[]{:S(2)}, u32[]{:S(2)}) %collective-permute-start.5) | collective-permute-done | bytes 262176 | tf_op jit(solution)/shard_map/ppermute | solution.py:98
  43.6 1.6 %collective-permute-start.11 = (bf16[4,256,256]{2,1,0:T(8,128)(2,1)}, bf16[4,256,256]{2,1,0:T(8,128)(2,1)}, u32[]{:S(2)}, u32[]{:S(2)}) collective-permute-start(bf16[4,256,256]{2,1,0:T(8,128)(2,1)} %collective-permute-done.9.refs_17_), channel_id=1, source_target_pairs={{0,64},{1,65},{2,66},{3,67},{4,68},{5,69},{6,70},{7,71},{8,72},{9,... | collective-permute-start | bytes 1572872 | tf_op jit(solution)/shard_map/ppermute | solution.py:98
  47.6 6.0 %collective-permute-done.17.refs_8_ = bf16[512,256]{1,0:T(8,128)(2,1)} collective-permute-done((bf16[512,256]{1,0:T(8,128)(2,1)}, bf16[512,256]{1,0:T(8,128)(2,1)}, u32[]{:S(2)}, u32[]{:S(2)}) %collective-permute-start.17) | collective-permute-done | bytes 262176 | tf_op jit(solution)/shard_map/ppermute | solution.py:98
  56.1 3.2 %shard_map.47 = bf16[512,256]{1,0:T(8,128)(2,1)S(1)} custom-call(s32[6]{0:T(128)S(1)} %stack.64.place, bf16[512,256]{1,0:T(8,128)(2,1)S(1)} %broadcast_select_fusion.3.refs_0_, bf16[512,256]{1,0:T(8,128)(2,1)} %collective-permute-done.13.refs_1_, bf16[512,256]{1,0:T(8,128)(2,1)S(1)} %collective-permute-done.1.refs_2_, ...), custom_call_target="tpu_custom_call" | custom-call | flops 1073741824 | bytes 6291456 | tf_op jit(solution)/shard_map/pallas_call | solution.py:213
  59.4 2.0 %collective-permute-start.25 = (bf16[512,256]{1,0:T(8,128)(2,1)S(1)}, bf16[512,256]{1,0:T(8,128)(2,1)S(1)}, u32[]{:S(2)}, u32[]{:S(2)}) collective-permute-start(bf16[512,256]{1,0:T(8,128)(2,1)S(1)} %shard_map.47), channel_id=1, source_target_pairs={{0,40},{1,41},{2,42},{3,43},{4,44},{5,45},{6,46},{7,47},{8,0},{9,1... | collective-permute-start | bytes 786440 | tf_op jit(solution)/shard_map/ppermute | solution.py:98
  61.4 2.2 %collective-permute-done.23 = bf16[256,1280]{1,0:T(8,128)(2,1)S(1)} collective-permute-done((bf16[256,1280]{1,0:T(8,128)(2,1)S(1)}, bf16[256,1280]{1,0:T(8,128)(2,1)S(1)}, u32[]{:S(2)}, u32[]{:S(2)}) %collective-permute-start.23) | collective-permute-done | bytes 655392 | tf_op jit(solution)/shard_map/ppermute | solution.py:98
  63.7 2.1 %collective-permute-done.22 = bf16[512,256]{1,0:T(8,128)(2,1)S(1)} collective-permute-done((bf16[512,256]{1,0:T(8,128)(2,1)S(1)}, bf16[512,256]{1,0:T(8,128)(2,1)S(1)}, u32[]{:S(2)}, u32[]{:S(2)}) %collective-permute-start.22) | collective-permute-done | bytes 262176 | tf_op jit(solution)/shard_map/ppermute | solution.py:98
  66.9 4.2 %shard_map.48.query = bf16[1024,128]{1,0:T(8,128)(2,1)S(1)} custom-call(s32[6]{0:T(128)S(1)} %stack.64.place, bf16[512,256]{1,0:T(8,128)(2,1)S(1)} %broadcast_select_fusion.3.refs_0_, bf16[512,256]{1,0:T(8,128)(2,1)} %collective-permute-done.13.refs_1_, bf16[512,256]{1,0:T(8,128)(2,1)S(1)} %collective-permute-done.1.refs_2_, ...), custom_call_target="tpu_custom_call" | custom-call | flops 1073741824 | bytes 6291456 | tf_op jit(solution)/shard_map/pallas_call | solution.py:228
  74.4 3.5 %shard_map.49 = (f32[1024,128]{1,0:T(8,128)S(1)}, f32[1024,128]{1,0:T(8,128)S(1)}, f32[1024,128]{1,0:T(8,128)S(1)}) custom-call(s32[6]{0:T(128)S(1)} %stack.64.place, bf16[1024,128]{1,0:T(8,128)(2,1)S(1)} %shard_map.48.query, bf16[4,512,256]{2,1,0:T(8,128)(2,1)S(1)} %pad_maximum_fusion.refs_0_), custom_call_target="tpu_custom_call" | custom-call | flops 1073741824 | bytes 1048576 | tf_op jit(solution)/shard_map/pallas_call | solution.py:328
  77.9 9.3 %collective-permute-done.26.refs_0_ = bf16[4,512,256]{2,1,0:T(8,128)(2,1)S(1)} collective-permute-done((bf16[4,512,256]{2,1,0:T(8,128)(2,1)S(1)}, bf16[4,512,256]{2,1,0:T(8,128)(2,1)S(1)}, u32[]{:S(2)}, u32[]{:S(2)}) %collective-permute-start.26) | collective-permute-done | bytes 1048608 | tf_op jit(solution)/shard_map/ppermute | solution.py:98
  87.9 3.4 %collective-permute-start.28 = (bf16[2,512,256]{2,1,0:T(8,128)(2,1)S(1)}, bf16[2,512,256]{2,1,0:T(8,128)(2,1)S(1)}, u32[]{:S(2)}, u32[]{:S(2)}) collective-permute-start(bf16[2,512,256]{2,1,0:T(8,128)(2,1)S(1)} %slice.62), channel_id=1, source_target_pairs={{0,64},{1,65},{2,66},{3,67},{4,68},{5,69},{6,70},{7,71},{8,72},{9,... | collective-permute-start | bytes 1572872 | tf_op jit(solution)/shard_map/ppermute | solution.py:98
  91.5 4.3 %shard_map.50 = (f32[1024,128]{1,0:T(8,128)S(1)}, f32[1024,128]{1,0:T(8,128)S(1)}, f32[1024,128]{1,0:T(8,128)S(1)}) custom-call(s32[6]{0:T(128)S(1)} %stack.64.place, bf16[1024,128]{1,0:T(8,128)(2,1)S(1)} %shard_map.48.query, bf16[4,512,256]{2,1,0:T(8,128)(2,1)S(1)} %collective-permute-done.26.refs_0_, ...), custom_call_target="tpu_custom_call" | custom-call | flops 2147483648 | bytes 2097152 | tf_op jit(solution)/shard_map/pallas_call | solution.py:328
  95.8 2.3 %collective-permute-done.28.refs_0_ = bf16[2,512,256]{2,1,0:T(8,128)(2,1)S(1)} collective-permute-done((bf16[2,512,256]{2,1,0:T(8,128)(2,1)S(1)}, bf16[2,512,256]{2,1,0:T(8,128)(2,1)S(1)}, u32[]{:S(2)}, u32[]{:S(2)}) %collective-permute-start.28) | collective-permute-done | bytes 524320 | tf_op jit(solution)/shard_map/ppermute | solution.py:98
  98.0 2.6 %collective-permute-done.29.refs_1_ = bf16[2,512,256]{2,1,0:T(8,128)(2,1)S(1)} collective-permute-done((bf16[2,512,256]{2,1,0:T(8,128)(2,1)S(1)}, bf16[2,512,256]{2,1,0:T(8,128)(2,1)S(1)}, u32[]{:S(2)}, u32[]{:S(2)}) %collective-permute-start.29) | collective-permute-done | bytes 524320 | tf_op jit(solution)/shard_map/ppermute | solution.py:98
  100.6 4.2 %shard_map.51 = bf16[512,256]{1,0:T(8,128)(2,1)S(1)} custom-call(s32[6]{0:T(128)S(1)} %stack.64.place, bf16[1024,128]{1,0:T(8,128)(2,1)S(1)} %shard_map.48.query, bf16[2,512,256]{2,1,0:T(8,128)(2,1)S(1)} %collective-permute-done.28.refs_0_, bf16[2,512,256]{2,1,0:T(8,128)(2,1)S(1)} %collective-permute-done.29.refs_1_, ...), custom_call_target="tpu_custom_call" | custom-call | flops 1073741824 | bytes 1048576 | tf_op jit(solution)/shard_map/pallas_call | solution.py:328
  104.9 1.7 %collective-permute-start.36 = (bf16[256,768]{1,0:T(8,128)(2,1)S(1)}, bf16[256,768]{1,0:T(8,128)(2,1)S(1)}, u32[]{:S(2)}, u32[]{:S(2)}) collective-permute-start(bf16[256,768]{1,0:T(8,128)(2,1)S(1)} %get-tuple-element.78), channel_id=1, source_target_pairs={{0,8},{1,9},{2,10},{3,11},{4,12},{5,13},{6,14},{7,15},{8,0},{9,1},... | collective-permute-start | bytes 1179656 | tf_op jit(solution)/shard_map/ppermute | solution.py:98
  109.3 1.7 %collective-permute-start.31 = (bf16[512,256]{1,0:T(8,128)(2,1)S(1)}, bf16[512,256]{1,0:T(8,128)(2,1)S(1)}, u32[]{:S(2)}, u32[]{:S(2)}) collective-permute-start(bf16[512,256]{1,0:T(8,128)(2,1)S(1)} %convolution_convert_fusion.2), channel_id=1, source_target_pairs={{0,1},{1,2},{2,3},{3,4},{4,5},{5,6},{6,7},{7,0},{8,9},{9,10},{10,1... | collective-permute-start | bytes 786440 | tf_op jit(solution)/shard_map/ppermute | solution.py:98
  111.9 5.4 %collective-permute-done.33 = bf16[512,256]{1,0:T(8,128)(2,1)S(1)} collective-permute-done((bf16[512,256]{1,0:T(8,128)(2,1)S(1)}, bf16[512,256]{1,0:T(8,128)(2,1)S(1)}, u32[]{:S(2)}, u32[]{:S(2)}) %collective-permute-start.33) | collective-permute-done | bytes 262176 | tf_op jit(solution)/shard_map/ppermute | solution.py:98
  118.4 1.7 %collective-permute-start.32 = (bf16[512,256]{1,0:T(8,128)(2,1)S(1)}, bf16[512,256]{1,0:T(8,128)(2,1)S(1)}, u32[]{:S(2)}, u32[]{:S(2)}) collective-permute-start(bf16[512,256]{1,0:T(8,128)(2,1)S(1)} %fusion), channel_id=1, source_target_pairs={{0,1},{1,2},{2,3},{3,4},{4,5},{5,6},{6,7},{7,0},{8,9},{9,10},{10,1... | collective-permute-start | bytes 786440 | tf_op jit(solution)/shard_map/ppermute | solution.py:98
  120.1 5.5 %collective-permute-done.34 = bf16[512,256]{1,0:T(8,128)(2,1)S(1)} collective-permute-done((bf16[512,256]{1,0:T(8,128)(2,1)S(1)}, bf16[512,256]{1,0:T(8,128)(2,1)S(1)}, u32[]{:S(2)}, u32[]{:S(2)}) %collective-permute-start.34) | collective-permute-done | bytes 262176 | tf_op jit(solution)/shard_map/ppermute | solution.py:98
  127.1 3.2 %collective-permute-start.37 = (bf16[512,256]{1,0:T(8,128)(2,1)S(1)}, bf16[512,256]{1,0:T(8,128)(2,1)S(1)}, u32[]{:S(2)}, u32[]{:S(2)}) collective-permute-start(bf16[512,256]{1,0:T(8,128)(2,1)S(1)} %fusion.2), channel_id=1, source_target_pairs={{0,7},{1,0},{2,1},{3,2},{4,3},{5,4},{6,5},{7,6},{8,23},{9,16},{10,... | collective-permute-start | bytes 786440 | tf_op jit(solution)/shard_map/ppermute | solution.py:98
  130.3 6.6 %collective-permute-done.38 = bf16[512,256]{1,0:T(8,128)(2,1)S(1)} collective-permute-done((bf16[512,256]{1,0:T(8,128)(2,1)S(1)}, bf16[512,256]{1,0:T(8,128)(2,1)S(1)}, u32[]{:S(2)}, u32[]{:S(2)}) %collective-permute-start.38) | collective-permute-done | bytes 262176 | tf_op jit(solution)/shard_map/ppermute | solution.py:98
  137.3 7.6 %collective-permute-done.39 = bf16[512,256]{1,0:T(8,128)(2,1)S(1)} collective-permute-done((bf16[512,256]{1,0:T(8,128)(2,1)S(1)}, bf16[512,256]{1,0:T(8,128)(2,1)S(1)}, u32[]{:S(2)}, u32[]{:S(2)}) %collective-permute-start.39) | collective-permute-done | bytes 262176 | tf_op jit(solution)/shard_map/ppermute | solution.py:98
  (107 shorter events, 25.3 us)
Async XLA Ops:
  0.0 10.3 %collective-permute-start = (bf16[512,256]{1,0:T(8,128)(2,1)}, bf16[512,256]{1,0:T(8,128)(2,1)}, u32[]{:S(2)}, u32[]{:S(2)}) collective-permute-start(bf16[512,256]{1,0:T(8,128)(2,1)} %param.4), channel_id=1, source_target_pairs={{8,16},{9,17},{10,18},{11,19},{12,20},{13,21},{14,22},{15,23},{16,... | collective-permute-start | bytes 786440 | tf_op jit(solution)/shard_map/ppermute | solution.py:98
  3.2 8.4 %collective-permute-start.3 = (bf16[2,256,256]{2,1,0:T(8,128)(2,1)}, bf16[2,256,256]{2,1,0:T(8,128)(2,1)S(1)}, u32[]{:S(2)}, u32[]{:S(2)}) collective-permute-start(bf16[2,256,256]{2,1,0:T(8,128)(2,1)} %pad_maximum_fusion.3), channel_id=1, source_target_pairs={{0,40},{1,41},{2,42},{3,43},{4,44},{5,45},{6,46},{7,47},{8,32},{9,... | collective-permute-start | bytes 786440 | tf_op jit(solution)/shard_map/ppermute | solution.py:98
  4.4 13.1 %collective-permute-start.1 = (bf16[512,256]{1,0:T(8,128)(2,1)}, bf16[512,256]{1,0:T(8,128)(2,1)S(1)}, u32[]{:S(2)}, u32[]{:S(2)}) collective-permute-start(bf16[512,256]{1,0:T(8,128)(2,1)} %param.4), channel_id=1, source_target_pairs={{0,1},{1,2},{2,3},{3,4},{4,5},{5,6},{6,7},{7,0},{8,23},{9,16},{10,... | collective-permute-start | bytes 786440 | tf_op jit(solution)/shard_map/ppermute | solution.py:98
  6.3 11.2 %collective-permute-start.2 = (bf16[512,256]{1,0:T(8,128)(2,1)}, bf16[512,256]{1,0:T(8,128)(2,1)S(1)}, u32[]{:S(2)}, u32[]{:S(2)}) collective-permute-start(bf16[512,256]{1,0:T(8,128)(2,1)} %param.4), channel_id=1, source_target_pairs={{0,7},{1,0},{2,1},{3,2},{4,3},{5,4},{6,5},{7,6},{8,17},{9,18},{10,... | collective-permute-start | bytes 786440 | tf_op jit(solution)/shard_map/ppermute | solution.py:98
  17.5 36.6 %collective-permute-start.12 = (bf16[4096,256]{1,0:T(8,128)(2,1)}, bf16[4096,256]{1,0:T(8,128)(2,1)}, u32[]{:S(2)}, u32[]{:S(2)}) collective-permute-start(bf16[4096,256]{1,0:T(8,128)(2,1)} %refs_16_), channel_id=1, source_target_pairs={{8,16},{9,17},{10,18},{11,19},{12,20},{13,21},{14,22},{15,23},{16,... | collective-permute-start | bytes 6291464 | tf_op jit(solution)/shard_map/ppermute | solution.py:98
  19.6 6.3 %collective-permute-start.8 = (bf16[2,256,256]{2,1,0:T(8,128)(2,1)S(1)}, bf16[2,256,256]{2,1,0:T(8,128)(2,1)S(1)}, u32[]{:S(2)}, u32[]{:S(2)}) collective-permute-start(bf16[2,256,256]{2,1,0:T(8,128)(2,1)S(1)} %pad_maximum_fusion.4), channel_id=1, source_target_pairs={{0,16},{1,17},{2,18},{3,19},{4,20},{5,21},{6,22},{7,23},{8,24},{9,... | collective-permute-start | bytes 786440 | tf_op jit(solution)/shard_map/ppermute | solution.py:98
  22.7 9.7 %collective-permute-start.4 = (bf16[512,256]{1,0:T(8,128)(2,1)S(1)}, bf16[512,256]{1,0:T(8,128)(2,1)S(1)}, u32[]{:S(2)}, u32[]{:S(2)}) collective-permute-start(bf16[512,256]{1,0:T(8,128)(2,1)S(1)} %collective-permute-done.1.refs_2_), channel_id=1, source_target_pairs={{0,1},{1,2},{2,3},{3,4},{4,5},{5,6},{6,7},{7,0},{8,9},{9,10},{10,1... | collective-permute-start | bytes 786440 | tf_op jit(solution)/shard_map/ppermute | solution.py:98
  22.7 9.7 %collective-permute-start.6 = (bf16[512,256]{1,0:T(8,128)(2,1)S(1)}, bf16[512,256]{1,0:T(8,128)(2,1)S(1)}, u32[]{:S(2)}, u32[]{:S(2)}) collective-permute-start(bf16[512,256]{1,0:T(8,128)(2,1)S(1)} %collective-permute-done.2.refs_14_), channel_id=1, source_target_pairs={{0,7},{1,0},{2,1},{3,2},{4,3},{5,4},{6,5},{7,6},{8,15},{9,8},{10,9... | collective-permute-start | bytes 786440 | tf_op jit(solution)/shard_map/ppermute | solution.py:98
  26.0 16.8 %collective-permute-start.10 = (bf16[4,256,256]{2,1,0:T(8,128)(2,1)S(1)}, bf16[4,256,256]{2,1,0:T(8,128)(2,1)S(1)}, u32[]{:S(2)}, u32[]{:S(2)}) collective-permute-start(bf16[4,256,256]{2,1,0:T(8,128)(2,1)S(1)} %pad_maximum_fusion.1.refs_16_), channel_id=1, source_target_pairs={{0,192},{1,193},{2,194},{3,195},{4,196},{5,197},{6,198},{7,199},{8... | collective-permute-start | bytes 1572872 | tf_op jit(solution)/shard_map/ppermute | solution.py:98
  26.5 16.3 %collective-permute-start.9 = (bf16[4,256,256]{2,1,0:T(8,128)(2,1)S(1)}, bf16[4,256,256]{2,1,0:T(8,128)(2,1)}, u32[]{:S(2)}, u32[]{:S(2)}) collective-permute-start(bf16[4,256,256]{2,1,0:T(8,128)(2,1)S(1)} %pad_maximum_fusion.1.refs_16_), channel_id=1, source_target_pairs={{0,64},{1,65},{2,66},{3,67},{4,68},{5,69},{6,70},{7,71},{8,72},{9,... | collective-permute-start | bytes 1572872 | tf_op jit(solution)/shard_map/ppermute | solution.py:98
  32.4 9.9 %collective-permute-start.5 = (bf16[512,256]{1,0:T(8,128)(2,1)S(1)}, bf16[512,256]{1,0:T(8,128)(2,1)S(1)}, u32[]{:S(2)}, u32[]{:S(2)}) collective-permute-start(bf16[512,256]{1,0:T(8,128)(2,1)S(1)} %collective-permute-done.4.refs_4_), channel_id=1, source_target_pairs={{0,1},{1,2},{2,3},{3,4},{4,5},{5,6},{6,7},{7,0},{8,9},{9,10},{10,1... | collective-permute-start | bytes 786440 | tf_op jit(solution)/shard_map/ppermute | solution.py:98
  32.4 9.9 %collective-permute-start.7 = (bf16[512,256]{1,0:T(8,128)(2,1)S(1)}, bf16[512,256]{1,0:T(8,128)(2,1)S(1)}, u32[]{:S(2)}, u32[]{:S(2)}) collective-permute-start(bf16[512,256]{1,0:T(8,128)(2,1)S(1)} %collective-permute-done.6.refs_12_), channel_id=1, source_target_pairs={{0,7},{1,0},{2,1},{3,2},{4,3},{5,4},{6,5},{7,6},{8,15},{9,8},{10,9... | collective-permute-start | bytes 786440 | tf_op jit(solution)/shard_map/ppermute | solution.py:98
  43.6 10.0 %collective-permute-start.11 = (bf16[4,256,256]{2,1,0:T(8,128)(2,1)}, bf16[4,256,256]{2,1,0:T(8,128)(2,1)}, u32[]{:S(2)}, u32[]{:S(2)}) collective-permute-start(bf16[4,256,256]{2,1,0:T(8,128)(2,1)} %collective-permute-done.9.refs_17_), channel_id=1, source_target_pairs={{0,64},{1,65},{2,66},{3,67},{4,68},{5,69},{6,70},{7,71},{8,72},{9,... | collective-permute-start | bytes 1572872 | tf_op jit(solution)/shard_map/ppermute | solution.py:98
  45.7 7.9 %collective-permute-start.17 = (bf16[512,256]{1,0:T(8,128)(2,1)}, bf16[512,256]{1,0:T(8,128)(2,1)}, u32[]{:S(2)}, u32[]{:S(2)}) collective-permute-start(bf16[512,256]{1,0:T(8,128)(2,1)} %copy-done.5), channel_id=1, source_target_pairs={{0,1},{1,2},{2,3},{3,4},{4,5},{5,6},{6,7},{7,0},{8,9},{9,10},{10,1... | collective-permute-start | bytes 786440 | tf_op jit(solution)/shard_map/ppermute | solution.py:98
  46.8 16.8 %collective-permute-start.23 = (bf16[256,1280]{1,0:T(8,128)(2,1)S(1)}, bf16[256,1280]{1,0:T(8,128)(2,1)S(1)}, u32[]{:S(2)}, u32[]{:S(2)}) collective-permute-start(bf16[256,1280]{1,0:T(8,128)(2,1)S(1)} %get-tuple-element.75), channel_id=1, source_target_pairs={{0,8},{1,9},{2,10},{3,11},{4,12},{5,13},{6,14},{7,15},{8,0},{9,1},... | collective-permute-start | bytes 1966088 | tf_op jit(solution)/shard_map/ppermute | solution.py:98
  47.4 8.0 %collective-permute-start.20 = (bf16[512,256]{1,0:T(8,128)(2,1)S(1)}, bf16[512,256]{1,0:T(8,128)(2,1)S(1)}, u32[]{:S(2)}, u32[]{:S(2)}) collective-permute-start(bf16[512,256]{1,0:T(8,128)(2,1)S(1)} %copy-done.4), channel_id=1, source_target_pairs={{0,16},{1,17},{2,18},{3,19},{4,20},{5,21},{6,22},{7,23},{8,24},{9,... | collective-permute-start | bytes 786440 | tf_op jit(solution)/shard_map/ppermute | solution.py:98
  59.3 6.4 %collective-permute-start.22 = (bf16[512,256]{1,0:T(8,128)(2,1)S(1)}, bf16[512,256]{1,0:T(8,128)(2,1)S(1)}, u32[]{:S(2)}, u32[]{:S(2)}) collective-permute-start(bf16[512,256]{1,0:T(8,128)(2,1)S(1)} %shard_map.47), channel_id=1, source_target_pairs={{0,8},{1,9},{2,10},{3,11},{4,12},{5,13},{6,14},{7,15},{8,32},{9,33... | collective-permute-start | bytes 786440 | tf_op jit(solution)/shard_map/ppermute | solution.py:98
  59.4 11.7 %collective-permute-start.25 = (bf16[512,256]{1,0:T(8,128)(2,1)S(1)}, bf16[512,256]{1,0:T(8,128)(2,1)S(1)}, u32[]{:S(2)}, u32[]{:S(2)}) collective-permute-start(bf16[512,256]{1,0:T(8,128)(2,1)S(1)} %shard_map.47), channel_id=1, source_target_pairs={{0,40},{1,41},{2,42},{3,43},{4,44},{5,45},{6,46},{7,47},{8,0},{9,1... | collective-permute-start | bytes 786440 | tf_op jit(solution)/shard_map/ppermute | solution.py:98
  65.8 6.4 %collective-permute-start.24 = (bf16[512,256]{1,0:T(8,128)(2,1)S(1)}, bf16[512,256]{1,0:T(8,128)(2,1)S(1)}, u32[]{:S(2)}, u32[]{:S(2)}) collective-permute-start(bf16[512,256]{1,0:T(8,128)(2,1)S(1)} %collective-permute-done.22), channel_id=1, source_target_pairs={{0,8},{1,9},{2,10},{3,11},{4,12},{5,13},{6,14},{7,15},{8,32},{9,33... | collective-permute-start | bytes 786440 | tf_op jit(solution)/shard_map/ppermute | solution.py:98
  72.3 14.9 %collective-permute-start.26 = (bf16[4,512,256]{2,1,0:T(8,128)(2,1)S(1)}, bf16[4,512,256]{2,1,0:T(8,128)(2,1)S(1)}, u32[]{:S(2)}, u32[]{:S(2)}) collective-permute-start(bf16[4,512,256]{2,1,0:T(8,128)(2,1)S(1)} %pad_maximum_fusion.refs_0_), channel_id=1, source_target_pairs={{0,64},{1,65},{2,66},{3,67},{4,68},{5,69},{6,70},{7,71},{8,72},{9,... | collective-permute-start | bytes 3145736 | tf_op jit(solution)/shard_map/ppermute | solution.py:98
  73.1 14.8 %collective-permute-start.27 = (bf16[4,512,256]{2,1,0:T(8,128)(2,1)S(1)}, bf16[4,512,256]{2,1,0:T(8,128)(2,1)S(1)}, u32[]{:S(2)}, u32[]{:S(2)}) collective-permute-start(bf16[4,512,256]{2,1,0:T(8,128)(2,1)S(1)} %pad_maximum_fusion.refs_0_), channel_id=1, source_target_pairs={{0,192},{1,193},{2,194},{3,195},{4,196},{5,197},{6,198},{7,199},{8... | collective-permute-start | bytes 3145736 | tf_op jit(solution)/shard_map/ppermute | solution.py:98
  87.9 10.1 %collective-permute-start.28 = (bf16[2,512,256]{2,1,0:T(8,128)(2,1)S(1)}, bf16[2,512,256]{2,1,0:T(8,128)(2,1)S(1)}, u32[]{:S(2)}, u32[]{:S(2)}) collective-permute-start(bf16[2,512,256]{2,1,0:T(8,128)(2,1)S(1)} %slice.62), channel_id=1, source_target_pairs={{0,64},{1,65},{2,66},{3,67},{4,68},{5,69},{6,70},{7,71},{8,72},{9,... | collective-permute-start | bytes 1572872 | tf_op jit(solution)/shard_map/ppermute | solution.py:98
  91.4 9.3 %collective-permute-start.29 = (bf16[2,512,256]{2,1,0:T(8,128)(2,1)S(1)}, bf16[2,512,256]{2,1,0:T(8,128)(2,1)S(1)}, u32[]{:S(2)}, u32[]{:S(2)}) collective-permute-start(bf16[2,512,256]{2,1,0:T(8,128)(2,1)S(1)} %slice.63), channel_id=1, source_target_pairs={{0,192},{1,193},{2,194},{3,195},{4,196},{5,197},{6,198},{7,199},{8... | collective-permute-start | bytes 1572872 | tf_op jit(solution)/shard_map/ppermute | solution.py:98
  104.9 15.2 %collective-permute-start.36 = (bf16[256,768]{1,0:T(8,128)(2,1)S(1)}, bf16[256,768]{1,0:T(8,128)(2,1)S(1)}, u32[]{:S(2)}, u32[]{:S(2)}) collective-permute-start(bf16[256,768]{1,0:T(8,128)(2,1)S(1)} %get-tuple-element.78), channel_id=1, source_target_pairs={{0,8},{1,9},{2,10},{3,11},{4,12},{5,13},{6,14},{7,15},{8,0},{9,1},... | collective-permute-start | bytes 1179656 | tf_op jit(solution)/shard_map/ppermute | solution.py:98
  108.4 8.8 %collective-permute-start.33 = (bf16[512,256]{1,0:T(8,128)(2,1)S(1)}, bf16[512,256]{1,0:T(8,128)(2,1)S(1)}, u32[]{:S(2)}, u32[]{:S(2)}) collective-permute-start(bf16[512,256]{1,0:T(8,128)(2,1)S(1)} %convolution_convert_fusion.1), channel_id=1, source_target_pairs={{0,7},{1,0},{2,1},{3,2},{4,3},{5,4},{6,5},{7,6},{8,15},{9,8},{10,9... | collective-permute-start | bytes 786440 | tf_op jit(solution)/shard_map/ppermute | solution.py:98
  109.3 8.8 %collective-permute-start.31 = (bf16[512,256]{1,0:T(8,128)(2,1)S(1)}, bf16[512,256]{1,0:T(8,128)(2,1)S(1)}, u32[]{:S(2)}, u32[]{:S(2)}) collective-permute-start(bf16[512,256]{1,0:T(8,128)(2,1)S(1)} %convolution_convert_fusion.2), channel_id=1, source_target_pairs={{0,1},{1,2},{2,3},{3,4},{4,5},{5,6},{6,7},{7,0},{8,9},{9,10},{10,1... | collective-permute-start | bytes 786440 | tf_op jit(solution)/shard_map/ppermute | solution.py:98
  111.2 8.9 %collective-permute-start.35 = (bf16[512,256]{1,0:T(8,128)(2,1)S(1)}, bf16[512,256]{1,0:T(8,128)(2,1)S(1)}, u32[]{:S(2)}, u32[]{:S(2)}) collective-permute-start(bf16[512,256]{1,0:T(8,128)(2,1)S(1)} %convolution_convert_fusion), channel_id=1, source_target_pairs={{8,16},{9,17},{10,18},{11,19},{12,20},{13,21},{14,22},{15,23},{16,... | collective-permute-start | bytes 786440 | tf_op jit(solution)/shard_map/ppermute | solution.py:98
  117.6 8.0 %collective-permute-start.34 = (bf16[512,256]{1,0:T(8,128)(2,1)S(1)}, bf16[512,256]{1,0:T(8,128)(2,1)S(1)}, u32[]{:S(2)}, u32[]{:S(2)}) collective-permute-start(bf16[512,256]{1,0:T(8,128)(2,1)S(1)} %fusion.1), channel_id=1, source_target_pairs={{0,7},{1,0},{2,1},{3,2},{4,3},{5,4},{6,5},{7,6},{8,15},{9,8},{10,9... | collective-permute-start | bytes 786440 | tf_op jit(solution)/shard_map/ppermute | solution.py:98
  118.4 7.9 %collective-permute-start.32 = (bf16[512,256]{1,0:T(8,128)(2,1)S(1)}, bf16[512,256]{1,0:T(8,128)(2,1)S(1)}, u32[]{:S(2)}, u32[]{:S(2)}) collective-permute-start(bf16[512,256]{1,0:T(8,128)(2,1)S(1)} %fusion), channel_id=1, source_target_pairs={{0,1},{1,2},{2,3},{3,4},{4,5},{5,6},{6,7},{7,0},{8,9},{9,10},{10,1... | collective-permute-start | bytes 786440 | tf_op jit(solution)/shard_map/ppermute | solution.py:98
  126.6 10.3 %collective-permute-start.38 = (bf16[512,256]{1,0:T(8,128)(2,1)S(1)}, bf16[512,256]{1,0:T(8,128)(2,1)S(1)}, u32[]{:S(2)}, u32[]{:S(2)}) collective-permute-start(bf16[512,256]{1,0:T(8,128)(2,1)S(1)} %fusion.4), channel_id=1, source_target_pairs={{0,1},{1,2},{2,3},{3,4},{4,5},{5,6},{6,7},{7,0},{8,9},{9,10},{10,1... | collective-permute-start | bytes 786440 | tf_op jit(solution)/shard_map/ppermute | solution.py:98
  127.1 10.2 %collective-permute-start.37 = (bf16[512,256]{1,0:T(8,128)(2,1)S(1)}, bf16[512,256]{1,0:T(8,128)(2,1)S(1)}, u32[]{:S(2)}, u32[]{:S(2)}) collective-permute-start(bf16[512,256]{1,0:T(8,128)(2,1)S(1)} %fusion.2), channel_id=1, source_target_pairs={{0,7},{1,0},{2,1},{3,2},{4,3},{5,4},{6,5},{7,6},{8,23},{9,16},{10,... | collective-permute-start | bytes 786440 | tf_op jit(solution)/shard_map/ppermute | solution.py:98
  137.2 7.7 %collective-permute-start.39 = (bf16[512,256]{1,0:T(8,128)(2,1)S(1)}, bf16[512,256]{1,0:T(8,128)(2,1)S(1)}, u32[]{:S(2)}, u32[]{:S(2)}) collective-permute-start(bf16[512,256]{1,0:T(8,128)(2,1)S(1)} %fusion.3), channel_id=1, source_target_pairs={{0,1},{1,2},{2,3},{3,4},{4,5},{5,6},{6,7},{7,0},{8,17},{9,18},{10,... | collective-permute-start | bytes 786440 | tf_op jit(solution)/shard_map/ppermute | solution.py:98
  (18 other events, 113.1 us)

commit v2 on v0

--- a/solution.py
+++ b/solution.py
@@ -386,9 +386,9 @@
     long = send(add(part_of(3), long), z_chain(1))
     short = send(add(part_of(6), short), z_chain(-1))
     middle = send_swapped(part_of(0).astype(jnp.bfloat16), same)
-    long, short, middle = lax.optimization_barrier((long, short, middle))
     long = send(add(part_of(2), long), z_chain(1))
     short = send(add(part_of(7), short), swap_back_route(-1))
+    long, middle = lax.optimization_barrier((long, middle))
     long = send(add(part_of(1), long), swap_back_route(1))
     total = middle.astype(jnp.float32) + short.astype(jnp.float32) + long.astype(jnp.float32)
     return total.astype(jnp.bfloat16)

time: 148 us -> 148 us (level); the launches traced: 146 us -> 148 us
  starting transfers between devices: 44.1 us -> 47.4 us
    ppermute x40, starting transfers between devices: 44.1 us -> 47.4 us  [send(): return lax.ppermute(value, BOTH, route)]
  transfers between devices with their start and end apart: 40 -> 40, of which waited for: 23 -> 22; matrix products, arithmetic and copies ran while one was open for 4% -> 5% of each run, Pallas kernels for 11% -> 11%
where the time goes in v2:
time: 148 us
  waiting for transfers between devices  71.1 us (48%)
  starting transfers between devices  47.4 us (32%)
  Pallas kernels  20.1 us (14%)
  other arithmetic  4.08 us (3%)
  matrix products  2.35 us (2%)
  local copies, waits for them, and re-layouts  2.19 us (1%)
    ppermute x40, waiting for transfers between devices, send(): return lax.ppermute(value, BOTH, route)  71.1 us
    ppermute x40, starting transfers between devices, send(): return lax.ppermute(value, BOTH, route)  47.4 us
    pallas_call x3, Pallas kernels, attend(): pl.pallas_call(functools.partial(attend_kernel, rows, steps, not state, l...  12 us
    pallas_call x1, Pallas kernels, project_q(): pl.pallas_call(functools.partial(project_q_kernel, rows), out_shape=jax.S...  4.21 us
    pallas_call x1, Pallas kernels, project_kv(): pl.pallas_call(project_kv_kernel, out_shape=jax.ShapeDtypeStruct((rows, 2...  3.22 us
  transfers between devices with their start and end apart: 40, of which 22 were waited for; matrix products, arithmetic and copies ran while one was open for 5% of the time, Pallas kernels for 11%

profile of v2, /device:TPU:20, one launch (start us, length us, event | category | flops | bytes accessed | tf_op | source)
XLA Modules:
  0.0 147.7 jit_solution(17642298232065425906)
XLA Ops:
  4.4 1.9 %collective-permute-start.1 = (bf16[512,256]{1,0:T(8,128)(2,1)}, bf16[512,256]{1,0:T(8,128)(2,1)S(1)}, u32[]{:S(2)}, u32[]{:S(2)}) collective-permute-start(bf16[512,256]{1,0:T(8,128)(2,1)} %param.4), channel_id=1, source_target_pairs={{0,1},{1,2},{2,3},{3,4},{4,5},{5,6},{6,7},{7,0},{8,23},{9,16},{10,... | collective-permute-start | bytes 786440 | tf_op jit(solution)/shard_map/ppermute | solution.py:98
  6.3 3.9 %collective-permute-start.2 = (bf16[512,256]{1,0:T(8,128)(2,1)}, bf16[512,256]{1,0:T(8,128)(2,1)S(1)}, u32[]{:S(2)}, u32[]{:S(2)}) collective-permute-start(bf16[512,256]{1,0:T(8,128)(2,1)} %param.4), channel_id=1, source_target_pairs={{0,7},{1,0},{2,1},{3,2},{4,3},{5,4},{6,5},{7,6},{8,17},{9,18},{10,... | collective-permute-start | bytes 786440 | tf_op jit(solution)/shard_map/ppermute | solution.py:98
  11.7 5.9 %collective-permute-done.1.refs_2_ = bf16[512,256]{1,0:T(8,128)(2,1)S(1)} collective-permute-done((bf16[512,256]{1,0:T(8,128)(2,1)}, bf16[512,256]{1,0:T(8,128)(2,1)S(1)}, u32[]{:S(2)}, u32[]{:S(2)}) %collective-permute-start.1) | collective-permute-done | bytes 262176 | tf_op jit(solution)/shard_map/ppermute | solution.py:98
  17.5 2.0 %collective-permute-start.12 = (bf16[4096,256]{1,0:T(8,128)(2,1)}, bf16[4096,256]{1,0:T(8,128)(2,1)}, u32[]{:S(2)}, u32[]{:S(2)}) collective-permute-start(bf16[4096,256]{1,0:T(8,128)(2,1)} %refs_16_), channel_id=1, source_target_pairs={{8,16},{9,17},{10,18},{11,19},{12,20},{13,21},{14,22},{15,23},{16,... | collective-permute-start | bytes 6291464 | tf_op jit(solution)/shard_map/ppermute | solution.py:98
  19.6 3.1 %collective-permute-start.8 = (bf16[2,256,256]{2,1,0:T(8,128)(2,1)S(1)}, bf16[2,256,256]{2,1,0:T(8,128)(2,1)S(1)}, u32[]{:S(2)}, u32[]{:S(2)}) collective-permute-start(bf16[2,256,256]{2,1,0:T(8,128)(2,1)S(1)} %pad_maximum_fusion.4), channel_id=1, source_target_pairs={{0,16},{1,17},{2,18},{3,19},{4,20},{5,21},{6,22},{7,23},{8,24},{9,... | collective-permute-start | bytes 786440 | tf_op jit(solution)/shard_map/ppermute | solution.py:98
  22.7 3.2 %collective-permute-start.6 = (bf16[512,256]{1,0:T(8,128)(2,1)S(1)}, bf16[512,256]{1,0:T(8,128)(2,1)S(1)}, u32[]{:S(2)}, u32[]{:S(2)}) collective-permute-start(bf16[512,256]{1,0:T(8,128)(2,1)S(1)} %collective-permute-done.2.refs_14_), channel_id=1, source_target_pairs={{0,7},{1,0},{2,1},{3,2},{4,3},{5,4},{6,5},{7,6},{8,15},{9,8},{10,9... | collective-permute-start | bytes 786440 | tf_op jit(solution)/shard_map/ppermute | solution.py:98
  26.5 1.6 %collective-permute-start.9 = (bf16[4,256,256]{2,1,0:T(8,128)(2,1)S(1)}, bf16[4,256,256]{2,1,0:T(8,128)(2,1)}, u32[]{:S(2)}, u32[]{:S(2)}) collective-permute-start(bf16[4,256,256]{2,1,0:T(8,128)(2,1)S(1)} %pad_maximum_fusion.1.refs_16_), channel_id=1, source_target_pairs={{0,64},{1,65},{2,66},{3,67},{4,68},{5,69},{6,70},{7,71},{8,72},{9,... | collective-permute-start | bytes 1572872 | tf_op jit(solution)/shard_map/ppermute | solution.py:98
  28.1 4.2 %collective-permute-done.4.refs_4_ = bf16[512,256]{1,0:T(8,128)(2,1)S(1)} collective-permute-done((bf16[512,256]{1,0:T(8,128)(2,1)S(1)}, bf16[512,256]{1,0:T(8,128)(2,1)S(1)}, u32[]{:S(2)}, u32[]{:S(2)}) %collective-permute-start.4) | collective-permute-done | bytes 262176 | tf_op jit(solution)/shard_map/ppermute | solution.py:98
  32.4 3.2 %collective-permute-start.7 = (bf16[512,256]{1,0:T(8,128)(2,1)S(1)}, bf16[512,256]{1,0:T(8,128)(2,1)S(1)}, u32[]{:S(2)}, u32[]{:S(2)}) collective-permute-start(bf16[512,256]{1,0:T(8,128)(2,1)S(1)} %collective-permute-done.6.refs_12_), channel_id=1, source_target_pairs={{0,7},{1,0},{2,1},{3,2},{4,3},{5,4},{6,5},{7,6},{8,15},{9,8},{10,9... | collective-permute-start | bytes 786440 | tf_op jit(solution)/shard_map/ppermute | solution.py:98
  35.6 6.7 %collective-permute-done.5.refs_6_ = bf16[512,256]{1,0:T(8,128)(2,1)S(1)} collective-permute-done((bf16[512,256]{1,0:T(8,128)(2,1)S(1)}, bf16[512,256]{1,0:T(8,128)(2,1)S(1)}, u32[]{:S(2)}, u32[]{:S(2)}) %collective-permute-start.5) | collective-permute-done | bytes 262176 | tf_op jit(solution)/shard_map/ppermute | solution.py:98
  43.6 1.6 %collective-permute-start.11 = (bf16[4,256,256]{2,1,0:T(8,128)(2,1)}, bf16[4,256,256]{2,1,0:T(8,128)(2,1)}, u32[]{:S(2)}, u32[]{:S(2)}) collective-permute-start(bf16[4,256,256]{2,1,0:T(8,128)(2,1)} %collective-permute-done.9.refs_17_), channel_id=1, source_target_pairs={{0,64},{1,65},{2,66},{3,67},{4,68},{5,69},{6,70},{7,71},{8,72},{9,... | collective-permute-start | bytes 1572872 | tf_op jit(solution)/shard_map/ppermute | solution.py:98
  47.6 6.0 %collective-permute-done.17.refs_8_ = bf16[512,256]{1,0:T(8,128)(2,1)} collective-permute-done((bf16[512,256]{1,0:T(8,128)(2,1)}, bf16[512,256]{1,0:T(8,128)(2,1)}, u32[]{:S(2)}, u32[]{:S(2)}) %collective-permute-start.17) | collective-permute-done | bytes 262176 | tf_op jit(solution)/shard_map/ppermute | solution.py:98
  56.1 3.2 %shard_map.47 = bf16[512,256]{1,0:T(8,128)(2,1)S(1)} custom-call(s32[6]{0:T(128)S(1)} %stack.64.place, bf16[512,256]{1,0:T(8,128)(2,1)S(1)} %broadcast_select_fusion.3.refs_0_, bf16[512,256]{1,0:T(8,128)(2,1)} %collective-permute-done.13.refs_1_, bf16[512,256]{1,0:T(8,128)(2,1)S(1)} %collective-permute-done.1.refs_2_, ...), custom_call_target="tpu_custom_call" | custom-call | flops 1073741824 | bytes 6291456 | tf_op jit(solution)/shard_map/pallas_call | solution.py:213
  59.4 2.0 %collective-permute-start.25 = (bf16[512,256]{1,0:T(8,128)(2,1)S(1)}, bf16[512,256]{1,0:T(8,128)(2,1)S(1)}, u32[]{:S(2)}, u32[]{:S(2)}) collective-permute-start(bf16[512,256]{1,0:T(8,128)(2,1)S(1)} %shard_map.47), channel_id=1, source_target_pairs={{0,40},{1,41},{2,42},{3,43},{4,44},{5,45},{6,46},{7,47},{8,0},{9,1... | collective-permute-start | bytes 786440 | tf_op jit(solution)/shard_map/ppermute | solution.py:98
  61.4 2.2 %collective-permute-done.23 = bf16[256,1280]{1,0:T(8,128)(2,1)S(1)} collective-permute-done((bf16[256,1280]{1,0:T(8,128)(2,1)S(1)}, bf16[256,1280]{1,0:T(8,128)(2,1)S(1)}, u32[]{:S(2)}, u32[]{:S(2)}) %collective-permute-start.23) | collective-permute-done | bytes 655392 | tf_op jit(solution)/shard_map/ppermute | solution.py:98
  63.7 2.1 %collective-permute-done.22 = bf16[512,256]{1,0:T(8,128)(2,1)S(1)} collective-permute-done((bf16[512,256]{1,0:T(8,128)(2,1)S(1)}, bf16[512,256]{1,0:T(8,128)(2,1)S(1)}, u32[]{:S(2)}, u32[]{:S(2)}) %collective-permute-start.22) | collective-permute-done | bytes 262176 | tf_op jit(solution)/shard_map/ppermute | solution.py:98
  66.9 4.2 %shard_map.48.query = bf16[1024,128]{1,0:T(8,128)(2,1)S(1)} custom-call(s32[6]{0:T(128)S(1)} %stack.64.place, bf16[512,256]{1,0:T(8,128)(2,1)S(1)} %broadcast_select_fusion.3.refs_0_, bf16[512,256]{1,0:T(8,128)(2,1)} %collective-permute-done.13.refs_1_, bf16[512,256]{1,0:T(8,128)(2,1)S(1)} %collective-permute-done.1.refs_2_, ...), custom_call_target="tpu_custom_call" | custom-call | flops 1073741824 | bytes 6291456 | tf_op jit(solution)/shard_map/pallas_call | solution.py:228
  74.4 3.5 %shard_map.49 = (f32[1024,128]{1,0:T(8,128)S(1)}, f32[1024,128]{1,0:T(8,128)S(1)}, f32[1024,128]{1,0:T(8,128)S(1)}) custom-call(s32[6]{0:T(128)S(1)} %stack.64.place, bf16[1024,128]{1,0:T(8,128)(2,1)S(1)} %shard_map.48.query, bf16[4,512,256]{2,1,0:T(8,128)(2,1)S(1)} %pad_maximum_fusion.refs_0_), custom_call_target="tpu_custom_call" | custom-call | flops 1073741824 | bytes 1048576 | tf_op jit(solution)/shard_map/pallas_call | solution.py:328
  77.9 9.3 %collective-permute-done.26.refs_0_ = bf16[4,512,256]{2,1,0:T(8,128)(2,1)S(1)} collective-permute-done((bf16[4,512,256]{2,1,0:T(8,128)(2,1)S(1)}, bf16[4,512,256]{2,1,0:T(8,128)(2,1)S(1)}, u32[]{:S(2)}, u32[]{:S(2)}) %collective-permute-start.26) | collective-permute-done | bytes 1048608 | tf_op jit(solution)/shard_map/ppermute | solution.py:98
  87.9 3.4 %collective-permute-start.28 = (bf16[2,512,256]{2,1,0:T(8,128)(2,1)S(1)}, bf16[2,512,256]{2,1,0:T(8,128)(2,1)S(1)}, u32[]{:S(2)}, u32[]{:S(2)}) collective-permute-start(bf16[2,512,256]{2,1,0:T(8,128)(2,1)S(1)} %slice.62), channel_id=1, source_target_pairs={{0,64},{1,65},{2,66},{3,67},{4,68},{5,69},{6,70},{7,71},{8,72},{9,... | collective-permute-start | bytes 1572872 | tf_op jit(solution)/shard_map/ppermute | solution.py:98
  91.5 4.3 %shard_map.50 = (f32[1024,128]{1,0:T(8,128)S(1)}, f32[1024,128]{1,0:T(8,128)S(1)}, f32[1024,128]{1,0:T(8,128)S(1)}) custom-call(s32[6]{0:T(128)S(1)} %stack.64.place, bf16[1024,128]{1,0:T(8,128)(2,1)S(1)} %shard_map.48.query, bf16[4,512,256]{2,1,0:T(8,128)(2,1)S(1)} %collective-permute-done.26.refs_0_, ...), custom_call_target="tpu_custom_call" | custom-call | flops 2147483648 | bytes 2097152 | tf_op jit(solution)/shard_map/pallas_call | solution.py:328
  95.8 2.3 %collective-permute-done.28.refs_0_ = bf16[2,512,256]{2,1,0:T(8,128)(2,1)S(1)} collective-permute-done((bf16[2,512,256]{2,1,0:T(8,128)(2,1)S(1)}, bf16[2,512,256]{2,1,0:T(8,128)(2,1)S(1)}, u32[]{:S(2)}, u32[]{:S(2)}) %collective-permute-start.28) | collective-permute-done | bytes 524320 | tf_op jit(solution)/shard_map/ppermute | solution.py:98
  98.0 2.6 %collective-permute-done.29.refs_1_ = bf16[2,512,256]{2,1,0:T(8,128)(2,1)S(1)} collective-permute-done((bf16[2,512,256]{2,1,0:T(8,128)(2,1)S(1)}, bf16[2,512,256]{2,1,0:T(8,128)(2,1)S(1)}, u32[]{:S(2)}, u32[]{:S(2)}) %collective-permute-start.29) | collective-permute-done | bytes 524320 | tf_op jit(solution)/shard_map/ppermute | solution.py:98
  100.6 4.2 %shard_map.51 = bf16[512,256]{1,0:T(8,128)(2,1)S(1)} custom-call(s32[6]{0:T(128)S(1)} %stack.64.place, bf16[1024,128]{1,0:T(8,128)(2,1)S(1)} %shard_map.48.query, bf16[2,512,256]{2,1,0:T(8,128)(2,1)S(1)} %collective-permute-done.28.refs_0_, bf16[2,512,256]{2,1,0:T(8,128)(2,1)S(1)} %collective-permute-done.29.refs_1_, ...), custom_call_target="tpu_custom_call" | custom-call | flops 1073741824 | bytes 1048576 | tf_op jit(solution)/shard_map/pallas_call | solution.py:328
  104.9 1.7 %collective-permute-start.31 = (bf16[256,768]{1,0:T(8,128)(2,1)S(1)}, bf16[256,768]{1,0:T(8,128)(2,1)S(1)}, u32[]{:S(2)}, u32[]{:S(2)}) collective-permute-start(bf16[256,768]{1,0:T(8,128)(2,1)S(1)} %get-tuple-element.74), channel_id=1, source_target_pairs={{0,8},{1,9},{2,10},{3,11},{4,12},{5,13},{6,14},{7,15},{8,0},{9,1},... | collective-permute-start | bytes 1179656 | tf_op jit(solution)/shard_map/ppermute | solution.py:98
  109.0 3.1 %collective-permute-start.36 = (bf16[512,256]{1,0:T(8,128)(2,1)S(1)}, bf16[512,256]{1,0:T(8,128)(2,1)S(1)}, u32[]{:S(2)}, u32[]{:S(2)}) collective-permute-start(bf16[512,256]{1,0:T(8,128)(2,1)S(1)} %convolution_convert_fusion), channel_id=1, source_target_pairs={{0,7},{1,0},{2,1},{3,2},{4,3},{5,4},{6,5},{7,6},{8,15},{9,8},{10,9... | collective-permute-start | bytes 786440 | tf_op jit(solution)/shard_map/ppermute | solution.py:98
  113.1 5.5 %collective-permute-done.32 = bf16[512,256]{1,0:T(8,128)(2,1)S(1)} collective-permute-done((bf16[512,256]{1,0:T(8,128)(2,1)S(1)}, bf16[512,256]{1,0:T(8,128)(2,1)S(1)}, u32[]{:S(2)}, u32[]{:S(2)}) %collective-permute-start.32) | collective-permute-done | bytes 262176 | tf_op jit(solution)/shard_map/ppermute | solution.py:98
  119.4 3.3 %collective-permute-start.37 = (bf16[512,256]{1,0:T(8,128)(2,1)S(1)}, bf16[512,256]{1,0:T(8,128)(2,1)S(1)}, u32[]{:S(2)}, u32[]{:S(2)}) collective-permute-start(bf16[512,256]{1,0:T(8,128)(2,1)S(1)} %fusion.3), channel_id=1, source_target_pairs={{0,7},{1,0},{2,1},{3,2},{4,3},{5,4},{6,5},{7,6},{8,15},{9,8},{10,9... | collective-permute-start | bytes 786440 | tf_op jit(solution)/shard_map/ppermute | solution.py:98
  122.6 5.6 %collective-permute-done.33 = bf16[512,256]{1,0:T(8,128)(2,1)S(1)} collective-permute-done((bf16[512,256]{1,0:T(8,128)(2,1)S(1)}, bf16[512,256]{1,0:T(8,128)(2,1)S(1)}, u32[]{:S(2)}, u32[]{:S(2)}) %collective-permute-start.33) | collective-permute-done | bytes 262176 | tf_op jit(solution)/shard_map/ppermute | solution.py:98
  129.0 3.8 %collective-permute-start.38 = (bf16[512,256]{1,0:T(8,128)(2,1)S(1)}, bf16[512,256]{1,0:T(8,128)(2,1)S(1)}, u32[]{:S(2)}, u32[]{:S(2)}) collective-permute-start(bf16[512,256]{1,0:T(8,128)(2,1)S(1)} %fusion.2), channel_id=1, source_target_pairs={{0,7},{1,0},{2,1},{3,2},{4,3},{5,4},{6,5},{7,6},{8,23},{9,16},{10,... | collective-permute-start | bytes 786440 | tf_op jit(solution)/shard_map/ppermute | solution.py:98
  132.8 6.2 %collective-permute-done.34 = bf16[512,256]{1,0:T(8,128)(2,1)S(1)} collective-permute-done((bf16[512,256]{1,0:T(8,128)(2,1)S(1)}, bf16[512,256]{1,0:T(8,128)(2,1)S(1)}, u32[]{:S(2)}, u32[]{:S(2)}) %collective-permute-start.34) | collective-permute-done | bytes 262176 | tf_op jit(solution)/shard_map/ppermute | solution.py:98
  139.4 7.6 %collective-permute-done.39 = bf16[512,256]{1,0:T(8,128)(2,1)S(1)} collective-permute-done((bf16[512,256]{1,0:T(8,128)(2,1)S(1)}, bf16[512,256]{1,0:T(8,128)(2,1)S(1)}, u32[]{:S(2)}, u32[]{:S(2)}) %collective-permute-start.39) | collective-permute-done | bytes 262176 | tf_op jit(solution)/shard_map/ppermute | solution.py:98
  (107 shorter events, 23.9 us)
Async XLA Ops:
  0.0 10.3 %collective-permute-start = (bf16[512,256]{1,0:T(8,128)(2,1)}, bf16[512,256]{1,0:T(8,128)(2,1)}, u32[]{:S(2)}, u32[]{:S(2)}) collective-permute-start(bf16[512,256]{1,0:T(8,128)(2,1)} %param.4), channel_id=1, source_target_pairs={{8,16},{9,17},{10,18},{11,19},{12,20},{13,21},{14,22},{15,23},{16,... | collective-permute-start | bytes 786440 | tf_op jit(solution)/shard_map/ppermute | solution.py:98
  3.2 8.4 %collective-permute-start.3 = (bf16[2,256,256]{2,1,0:T(8,128)(2,1)}, bf16[2,256,256]{2,1,0:T(8,128)(2,1)S(1)}, u32[]{:S(2)}, u32[]{:S(2)}) collective-permute-start(bf16[2,256,256]{2,1,0:T(8,128)(2,1)} %pad_maximum_fusion.3), channel_id=1, source_target_pairs={{0,40},{1,41},{2,42},{3,43},{4,44},{5,45},{6,46},{7,47},{8,32},{9,... | collective-permute-start | bytes 786440 | tf_op jit(solution)/shard_map/ppermute | solution.py:98
  4.4 13.1 %collective-permute-start.1 = (bf16[512,256]{1,0:T(8,128)(2,1)}, bf16[512,256]{1,0:T(8,128)(2,1)S(1)}, u32[]{:S(2)}, u32[]{:S(2)}) collective-permute-start(bf16[512,256]{1,0:T(8,128)(2,1)} %param.4), channel_id=1, source_target_pairs={{0,1},{1,2},{2,3},{3,4},{4,5},{5,6},{6,7},{7,0},{8,23},{9,16},{10,... | collective-permute-start | bytes 786440 | tf_op jit(solution)/shard_map/ppermute | solution.py:98
  6.3 11.2 %collective-permute-start.2 = (bf16[512,256]{1,0:T(8,128)(2,1)}, bf16[512,256]{1,0:T(8,128)(2,1)S(1)}, u32[]{:S(2)}, u32[]{:S(2)}) collective-permute-start(bf16[512,256]{1,0:T(8,128)(2,1)} %param.4), channel_id=1, source_target_pairs={{0,7},{1,0},{2,1},{3,2},{4,3},{5,4},{6,5},{7,6},{8,17},{9,18},{10,... | collective-permute-start | bytes 786440 | tf_op jit(solution)/shard_map/ppermute | solution.py:98
  17.5 36.6 %collective-permute-start.12 = (bf16[4096,256]{1,0:T(8,128)(2,1)}, bf16[4096,256]{1,0:T(8,128)(2,1)}, u32[]{:S(2)}, u32[]{:S(2)}) collective-permute-start(bf16[4096,256]{1,0:T(8,128)(2,1)} %refs_16_), channel_id=1, source_target_pairs={{8,16},{9,17},{10,18},{11,19},{12,20},{13,21},{14,22},{15,23},{16,... | collective-permute-start | bytes 6291464 | tf_op jit(solution)/shard_map/ppermute | solution.py:98
  19.6 6.3 %collective-permute-start.8 = (bf16[2,256,256]{2,1,0:T(8,128)(2,1)S(1)}, bf16[2,256,256]{2,1,0:T(8,128)(2,1)S(1)}, u32[]{:S(2)}, u32[]{:S(2)}) collective-permute-start(bf16[2,256,256]{2,1,0:T(8,128)(2,1)S(1)} %pad_maximum_fusion.4), channel_id=1, source_target_pairs={{0,16},{1,17},{2,18},{3,19},{4,20},{5,21},{6,22},{7,23},{8,24},{9,... | collective-permute-start | bytes 786440 | tf_op jit(solution)/shard_map/ppermute | solution.py:98
  22.7 9.7 %collective-permute-start.4 = (bf16[512,256]{1,0:T(8,128)(2,1)S(1)}, bf16[512,256]{1,0:T(8,128)(2,1)S(1)}, u32[]{:S(2)}, u32[]{:S(2)}) collective-permute-start(bf16[512,256]{1,0:T(8,128)(2,1)S(1)} %collective-permute-done.1.refs_2_), channel_id=1, source_target_pairs={{0,1},{1,2},{2,3},{3,4},{4,5},{5,6},{6,7},{7,0},{8,9},{9,10},{10,1... | collective-permute-start | bytes 786440 | tf_op jit(solution)/shard_map/ppermute | solution.py:98
  22.7 9.7 %collective-permute-start.6 = (bf16[512,256]{1,0:T(8,128)(2,1)S(1)}, bf16[512,256]{1,0:T(8,128)(2,1)S(1)}, u32[]{:S(2)}, u32[]{:S(2)}) collective-permute-start(bf16[512,256]{1,0:T(8,128)(2,1)S(1)} %collective-permute-done.2.refs_14_), channel_id=1, source_target_pairs={{0,7},{1,0},{2,1},{3,2},{4,3},{5,4},{6,5},{7,6},{8,15},{9,8},{10,9... | collective-permute-start | bytes 786440 | tf_op jit(solution)/shard_map/ppermute | solution.py:98
  26.0 16.8 %collective-permute-start.10 = (bf16[4,256,256]{2,1,0:T(8,128)(2,1)S(1)}, bf16[4,256,256]{2,1,0:T(8,128)(2,1)S(1)}, u32[]{:S(2)}, u32[]{:S(2)}) collective-permute-start(bf16[4,256,256]{2,1,0:T(8,128)(2,1)S(1)} %pad_maximum_fusion.1.refs_16_), channel_id=1, source_target_pairs={{0,192},{1,193},{2,194},{3,195},{4,196},{5,197},{6,198},{7,199},{8... | collective-permute-start | bytes 1572872 | tf_op jit(solution)/shard_map/ppermute | solution.py:98
  26.5 16.3 %collective-permute-start.9 = (bf16[4,256,256]{2,1,0:T(8,128)(2,1)S(1)}, bf16[4,256,256]{2,1,0:T(8,128)(2,1)}, u32[]{:S(2)}, u32[]{:S(2)}) collective-permute-start(bf16[4,256,256]{2,1,0:T(8,128)(2,1)S(1)} %pad_maximum_fusion.1.refs_16_), channel_id=1, source_target_pairs={{0,64},{1,65},{2,66},{3,67},{4,68},{5,69},{6,70},{7,71},{8,72},{9,... | collective-permute-start | bytes 1572872 | tf_op jit(solution)/shard_map/ppermute | solution.py:98
  32.4 9.9 %collective-permute-start.5 = (bf16[512,256]{1,0:T(8,128)(2,1)S(1)}, bf16[512,256]{1,0:T(8,128)(2,1)S(1)}, u32[]{:S(2)}, u32[]{:S(2)}) collective-permute-start(bf16[512,256]{1,0:T(8,128)(2,1)S(1)} %collective-permute-done.4.refs_4_), channel_id=1, source_target_pairs={{0,1},{1,2},{2,3},{3,4},{4,5},{5,6},{6,7},{7,0},{8,9},{9,10},{10,1... | collective-permute-start | bytes 786440 | tf_op jit(solution)/shard_map/ppermute | solution.py:98
  32.4 9.9 %collective-permute-start.7 = (bf16[512,256]{1,0:T(8,128)(2,1)S(1)}, bf16[512,256]{1,0:T(8,128)(2,1)S(1)}, u32[]{:S(2)}, u32[]{:S(2)}) collective-permute-start(bf16[512,256]{1,0:T(8,128)(2,1)S(1)} %collective-permute-done.6.refs_12_), channel_id=1, source_target_pairs={{0,7},{1,0},{2,1},{3,2},{4,3},{5,4},{6,5},{7,6},{8,15},{9,8},{10,9... | collective-permute-start | bytes 786440 | tf_op jit(solution)/shard_map/ppermute | solution.py:98
  43.6 10.0 %collective-permute-start.11 = (bf16[4,256,256]{2,1,0:T(8,128)(2,1)}, bf16[4,256,256]{2,1,0:T(8,128)(2,1)}, u32[]{:S(2)}, u32[]{:S(2)}) collective-permute-start(bf16[4,256,256]{2,1,0:T(8,128)(2,1)} %collective-permute-done.9.refs_17_), channel_id=1, source_target_pairs={{0,64},{1,65},{2,66},{3,67},{4,68},{5,69},{6,70},{7,71},{8,72},{9,... | collective-permute-start | bytes 1572872 | tf_op jit(solution)/shard_map/ppermute | solution.py:98
  45.7 7.9 %collective-permute-start.17 = (bf16[512,256]{1,0:T(8,128)(2,1)}, bf16[512,256]{1,0:T(8,128)(2,1)}, u32[]{:S(2)}, u32[]{:S(2)}) collective-permute-start(bf16[512,256]{1,0:T(8,128)(2,1)} %copy-done.5), channel_id=1, source_target_pairs={{0,1},{1,2},{2,3},{3,4},{4,5},{5,6},{6,7},{7,0},{8,9},{9,10},{10,1... | collective-permute-start | bytes 786440 | tf_op jit(solution)/shard_map/ppermute | solution.py:98
  46.8 16.8 %collective-permute-start.23 = (bf16[256,1280]{1,0:T(8,128)(2,1)S(1)}, bf16[256,1280]{1,0:T(8,128)(2,1)S(1)}, u32[]{:S(2)}, u32[]{:S(2)}) collective-permute-start(bf16[256,1280]{1,0:T(8,128)(2,1)S(1)} %get-tuple-element.75), channel_id=1, source_target_pairs={{0,8},{1,9},{2,10},{3,11},{4,12},{5,13},{6,14},{7,15},{8,0},{9,1},... | collective-permute-start | bytes 1966088 | tf_op jit(solution)/shard_map/ppermute | solution.py:98
  47.4 8.0 %collective-permute-start.20 = (bf16[512,256]{1,0:T(8,128)(2,1)S(1)}, bf16[512,256]{1,0:T(8,128)(2,1)S(1)}, u32[]{:S(2)}, u32[]{:S(2)}) collective-permute-start(bf16[512,256]{1,0:T(8,128)(2,1)S(1)} %copy-done.4), channel_id=1, source_target_pairs={{0,16},{1,17},{2,18},{3,19},{4,20},{5,21},{6,22},{7,23},{8,24},{9,... | collective-permute-start | bytes 786440 | tf_op jit(solution)/shard_map/ppermute | solution.py:98
  59.3 6.4 %collective-permute-start.22 = (bf16[512,256]{1,0:T(8,128)(2,1)S(1)}, bf16[512,256]{1,0:T(8,128)(2,1)S(1)}, u32[]{:S(2)}, u32[]{:S(2)}) collective-permute-start(bf16[512,256]{1,0:T(8,128)(2,1)S(1)} %shard_map.47), channel_id=1, source_target_pairs={{0,8},{1,9},{2,10},{3,11},{4,12},{5,13},{6,14},{7,15},{8,32},{9,33... | collective-permute-start | bytes 786440 | tf_op jit(solution)/shard_map/ppermute | solution.py:98
  59.4 11.7 %collective-permute-start.25 = (bf16[512,256]{1,0:T(8,128)(2,1)S(1)}, bf16[512,256]{1,0:T(8,128)(2,1)S(1)}, u32[]{:S(2)}, u32[]{:S(2)}) collective-permute-start(bf16[512,256]{1,0:T(8,128)(2,1)S(1)} %shard_map.47), channel_id=1, source_target_pairs={{0,40},{1,41},{2,42},{3,43},{4,44},{5,45},{6,46},{7,47},{8,0},{9,1... | collective-permute-start | bytes 786440 | tf_op jit(solution)/shard_map/ppermute | solution.py:98
  65.8 6.4 %collective-permute-start.24 = (bf16[512,256]{1,0:T(8,128)(2,1)S(1)}, bf16[512,256]{1,0:T(8,128)(2,1)S(1)}, u32[]{:S(2)}, u32[]{:S(2)}) collective-permute-start(bf16[512,256]{1,0:T(8,128)(2,1)S(1)} %collective-permute-done.22), channel_id=1, source_target_pairs={{0,8},{1,9},{2,10},{3,11},{4,12},{5,13},{6,14},{7,15},{8,32},{9,33... | collective-permute-start | bytes 786440 | tf_op jit(solution)/shard_map/ppermute | solution.py:98
  72.3 14.9 %collective-permute-start.26 = (bf16[4,512,256]{2,1,0:T(8,128)(2,1)S(1)}, bf16[4,512,256]{2,1,0:T(8,128)(2,1)S(1)}, u32[]{:S(2)}, u32[]{:S(2)}) collective-permute-start(bf16[4,512,256]{2,1,0:T(8,128)(2,1)S(1)} %pad_maximum_fusion.refs_0_), channel_id=1, source_target_pairs={{0,64},{1,65},{2,66},{3,67},{4,68},{5,69},{6,70},{7,71},{8,72},{9,... | collective-permute-start | bytes 3145736 | tf_op jit(solution)/shard_map/ppermute | solution.py:98
  73.1 14.8 %collective-permute-start.27 = (bf16[4,512,256]{2,1,0:T(8,128)(2,1)S(1)}, bf16[4,512,256]{2,1,0:T(8,128)(2,1)S(1)}, u32[]{:S(2)}, u32[]{:S(2)}) collective-permute-start(bf16[4,512,256]{2,1,0:T(8,128)(2,1)S(1)} %pad_maximum_fusion.refs_0_), channel_id=1, source_target_pairs={{0,192},{1,193},{2,194},{3,195},{4,196},{5,197},{6,198},{7,199},{8... | collective-permute-start | bytes 3145736 | tf_op jit(solution)/shard_map/ppermute | solution.py:98
  87.9 10.1 %collective-permute-start.28 = (bf16[2,512,256]{2,1,0:T(8,128)(2,1)S(1)}, bf16[2,512,256]{2,1,0:T(8,128)(2,1)S(1)}, u32[]{:S(2)}, u32[]{:S(2)}) collective-permute-start(bf16[2,512,256]{2,1,0:T(8,128)(2,1)S(1)} %slice.62), channel_id=1, source_target_pairs={{0,64},{1,65},{2,66},{3,67},{4,68},{5,69},{6,70},{7,71},{8,72},{9,... | collective-permute-start | bytes 1572872 | tf_op jit(solution)/shard_map/ppermute | solution.py:98
  91.4 9.3 %collective-permute-start.29 = (bf16[2,512,256]{2,1,0:T(8,128)(2,1)S(1)}, bf16[2,512,256]{2,1,0:T(8,128)(2,1)S(1)}, u32[]{:S(2)}, u32[]{:S(2)}) collective-permute-start(bf16[2,512,256]{2,1,0:T(8,128)(2,1)S(1)} %slice.63), channel_id=1, source_target_pairs={{0,192},{1,193},{2,194},{3,195},{4,196},{5,197},{6,198},{7,199},{8... | collective-permute-start | bytes 1572872 | tf_op jit(solution)/shard_map/ppermute | solution.py:98
  104.9 14.1 %collective-permute-start.31 = (bf16[256,768]{1,0:T(8,128)(2,1)S(1)}, bf16[256,768]{1,0:T(8,128)(2,1)S(1)}, u32[]{:S(2)}, u32[]{:S(2)}) collective-permute-start(bf16[256,768]{1,0:T(8,128)(2,1)S(1)} %get-tuple-element.74), channel_id=1, source_target_pairs={{0,8},{1,9},{2,10},{3,11},{4,12},{5,13},{6,14},{7,15},{8,0},{9,1},... | collective-permute-start | bytes 1179656 | tf_op jit(solution)/shard_map/ppermute | solution.py:98
  108.4 10.2 %collective-permute-start.32 = (bf16[512,256]{1,0:T(8,128)(2,1)S(1)}, bf16[512,256]{1,0:T(8,128)(2,1)S(1)}, u32[]{:S(2)}, u32[]{:S(2)}) collective-permute-start(bf16[512,256]{1,0:T(8,128)(2,1)S(1)} %convolution_convert_fusion.2), channel_id=1, source_target_pairs={{0,1},{1,2},{2,3},{3,4},{4,5},{5,6},{6,7},{7,0},{8,9},{9,10},{10,1... | collective-permute-start | bytes 786440 | tf_op jit(solution)/shard_map/ppermute | solution.py:98
  109.0 10.0 %collective-permute-start.36 = (bf16[512,256]{1,0:T(8,128)(2,1)S(1)}, bf16[512,256]{1,0:T(8,128)(2,1)S(1)}, u32[]{:S(2)}, u32[]{:S(2)}) collective-permute-start(bf16[512,256]{1,0:T(8,128)(2,1)S(1)} %convolution_convert_fusion), channel_id=1, source_target_pairs={{0,7},{1,0},{2,1},{3,2},{4,3},{5,4},{6,5},{7,6},{8,15},{9,8},{10,9... | collective-permute-start | bytes 786440 | tf_op jit(solution)/shard_map/ppermute | solution.py:98
  112.4 16.2 %collective-permute-start.35 = (bf16[512,256]{1,0:T(8,128)(2,1)S(1)}, bf16[512,256]{1,0:T(8,128)(2,1)S(1)}, u32[]{:S(2)}, u32[]{:S(2)}) collective-permute-start(bf16[512,256]{1,0:T(8,128)(2,1)S(1)} %convolution_convert_fusion.1), channel_id=1, source_target_pairs={{8,16},{9,17},{10,18},{11,19},{12,20},{13,21},{14,22},{15,23},{16,... | collective-permute-start | bytes 786440 | tf_op jit(solution)/shard_map/ppermute | solution.py:98
  118.9 9.3 %collective-permute-start.33 = (bf16[512,256]{1,0:T(8,128)(2,1)S(1)}, bf16[512,256]{1,0:T(8,128)(2,1)S(1)}, u32[]{:S(2)}, u32[]{:S(2)}) collective-permute-start(bf16[512,256]{1,0:T(8,128)(2,1)S(1)} %fusion.1), channel_id=1, source_target_pairs={{0,1},{1,2},{2,3},{3,4},{4,5},{5,6},{6,7},{7,0},{8,9},{9,10},{10,1... | collective-permute-start | bytes 786440 | tf_op jit(solution)/shard_map/ppermute | solution.py:98
  119.4 9.4 %collective-permute-start.37 = (bf16[512,256]{1,0:T(8,128)(2,1)S(1)}, bf16[512,256]{1,0:T(8,128)(2,1)S(1)}, u32[]{:S(2)}, u32[]{:S(2)}) collective-permute-start(bf16[512,256]{1,0:T(8,128)(2,1)S(1)} %fusion.3), channel_id=1, source_target_pairs={{0,7},{1,0},{2,1},{3,2},{4,3},{5,4},{6,5},{7,6},{8,15},{9,8},{10,9... | collective-permute-start | bytes 786440 | tf_op jit(solution)/shard_map/ppermute | solution.py:98
  128.5 10.5 %collective-permute-start.34 = (bf16[512,256]{1,0:T(8,128)(2,1)S(1)}, bf16[512,256]{1,0:T(8,128)(2,1)S(1)}, u32[]{:S(2)}, u32[]{:S(2)}) collective-permute-start(bf16[512,256]{1,0:T(8,128)(2,1)S(1)} %fusion), channel_id=1, source_target_pairs={{0,1},{1,2},{2,3},{3,4},{4,5},{5,6},{6,7},{7,0},{8,9},{9,10},{10,1... | collective-permute-start | bytes 786440 | tf_op jit(solution)/shard_map/ppermute | solution.py:98
  129.0 10.3 %collective-permute-start.38 = (bf16[512,256]{1,0:T(8,128)(2,1)S(1)}, bf16[512,256]{1,0:T(8,128)(2,1)S(1)}, u32[]{:S(2)}, u32[]{:S(2)}) collective-permute-start(bf16[512,256]{1,0:T(8,128)(2,1)S(1)} %fusion.2), channel_id=1, source_target_pairs={{0,7},{1,0},{2,1},{3,2},{4,3},{5,4},{6,5},{7,6},{8,23},{9,16},{10,... | collective-permute-start | bytes 786440 | tf_op jit(solution)/shard_map/ppermute | solution.py:98
  139.3 7.7 %collective-permute-start.39 = (bf16[512,256]{1,0:T(8,128)(2,1)S(1)}, bf16[512,256]{1,0:T(8,128)(2,1)S(1)}, u32[]{:S(2)}, u32[]{:S(2)}) collective-permute-start(bf16[512,256]{1,0:T(8,128)(2,1)S(1)} %fusion.4), channel_id=1, source_target_pairs={{0,1},{1,2},{2,3},{3,4},{4,5},{5,6},{6,7},{7,0},{8,17},{9,18},{10,... | collective-permute-start | bytes 786440 | tf_op jit(solution)/shard_map/ppermute | solution.py:98
  (18 other events, 113.1 us)
